TPU v7x, 256 devices: a whole 4x4x8 slice. The times are simulated.
256 devices in a mesh: span: 16 (over z, x_hi), mp: 16 (over y, x_lo, core).
Axes of the slice: x: 4 (x_hi: 2, x_lo: 2; x = x_hi * 2 + x_lo), y: 4, z: 8, core: 2. Of those that a mesh axis runs over, the one named last changes fastest.
Arguments:
- queries: bfloat16 [12288, 6144], P('span', 'mp'), may hold values from -11 to 11
- keys: bfloat16 [12288, 6144], P('span', 'mp'), may hold values from -11 to 11
- values: bfloat16 [12288, 6144], P('span', 'mp'), may hold values from -6 to 6
- residual: bfloat16 [12288, 6144], P(('span', 'mp')), may hold values from -6 to 6
- out_weight: bfloat16 [6144, 6144], P('mp'), may hold values from -0.078125 to 0.078125
- gate_table: float32 [16, 6144], replicated, may hold values from 0.5 to 2
- noise_steps: int32 [16], replicated, may hold values from 0 to 15, each once
- windows: int32 [16, 2], replicated, may hold values 0 or 1
Outputs:
- mixed: bfloat16 [12288, 6144], P(('span', 'mp'))
All inputs are finite; a program needn't handle non-finite values.
Results may differ from a plain program's by a relative error of at most 0.018.
Values may be sent and summed in bfloat16 or wider, within the bound.
No kernel may reach another device: no remote copies, remote signals or barrier semaphores. Data moves between devices by JAX's collectives and lax.ppermute only.
A program may use at most 64 MiB of HBM per device.

v0:
```python
import functools
import math

import jax
import jax.numpy as jnp
from jax import lax
from jax.experimental import pallas as pl
from jax.experimental.pallas import tpu as pltpu
from jax.sharding import Mesh, PartitionSpec as P

HD = 128
HEADS_HERE = 3
NZ, NXH, NY, NXL, NC = 8, 2, 4, 2, 2
X_FIRST = 2688
CHUNK = 16
UP = 2
LOG2E = math.log2(math.e)
SWAP = [(0, 1), (1, 0)]


def shift(value, axis, count, steps):
    return lax.ppermute(value, axis, [(i, (i + steps) % count) for i in range(count)])


def attend_body(fresh, last, flags, *refs):
    refs = list(refs)
    scalar_ref, q_ref = refs.pop(0), refs.pop(0)
    scores_ref, probs_ref = refs.pop(), refs.pop()
    if last:
        clean = (refs.pop(), refs.pop())
        peak_ref, total_ref, out_ref = refs.pop(), refs.pop(), refs.pop()
    else:
        total_ref, peak_ref = refs.pop(), refs.pop()
    if not fresh:
        old_total_ref, old_peak_ref = refs.pop(), refs.pop()
        peak_ref[...] = old_peak_ref[...]
        total_ref[...] = old_total_ref[...]
    if last:
        pieces = refs
        piece_rows = pieces[0].shape[1]

        @pl.when(pl.program_id(0) == 0)
        def _():
            for number, piece in enumerate(pieces):
                for side in range(2):
                    clean[side][pl.ds(number * piece_rows, piece_rows)] = piece[side]

        blocks = [clean]
    else:
        blocks = list(zip(refs[::2], refs[1::2]))
    factor = HD ** (-0.5) * LOG2E
    tile = probs_ref.shape[1]
    ones = jnp.ones((blocks[0][0].shape[0], HD), jnp.bfloat16)
    y, xl, core = scalar_ref[4], scalar_ref[5], scalar_ref[6]
    places = []
    for xl_step in range(NXL):
        for y_step in range(NY):
            y_there = lax.rem(y + y_step, NY)
            xl_there = lax.rem(xl + xl_step, NXL)
            places.append((y_there * NXL + xl_there) * NC + lax.rem(core + pl.program_id(0), NC))

    def one_block(first, k_ref, v_ref):
        def take_scores(head):
            cols = slice(head * HD, (head + 1) * HD)
            rows = jnp.concatenate([q_ref[place, :, cols] for place in places], axis=0)
            scores_ref[head % 2] = lax.dot_general(
                rows, k_ref[:, cols], (((1,), (1,)), ((), ())), preferred_element_type=jnp.float32
            )

        take_scores(0)
        for head in range(HEADS_HERE):
            cols = slice(head * HD, (head + 1) * HD)
            if head + 1 < HEADS_HERE:
                take_scores(head + 1)
            scales = []
            for low in range(0, tile, CHUNK):
                rows = slice(low, low + CHUNK)
                scores = scores_ref[head % 2, rows]
                peak = jnp.max(scores, axis=1, keepdims=True)
                if not first:
                    old_peak = peak_ref[head, rows]
                    peak = jnp.maximum(old_peak, peak)
                    scales.append(jnp.exp2((old_peak - peak) * factor))
                probs_ref[head % 2, rows] = jnp.exp2(((scores - peak) * factor).astype(jnp.bfloat16))
                peak_ref[head, rows] = peak
            wide = jnp.concatenate([v_ref[:, cols], ones], axis=1)
            added = jnp.dot(probs_ref[head % 2], wide, preferred_element_type=jnp.float32)
            total_ref[head] = added if first else total_ref[head] * jnp.concatenate(scales, axis=0) + added

    for number, (k_ref, v_ref) in enumerate(blocks):
        if fresh and number == 0:
            one_block(True, k_ref, v_ref)
        else:
            pl.when(scalar_ref[flags[number]] == 1)(functools.partial(one_block, False, k_ref, v_ref))
    if last:
        for head in range(HEADS_HERE):
            total = total_ref[head]
            out_ref[:, head * HD : (head + 1) * HD] = (total[:, :HD] / total[:, HD:]).astype(jnp.bfloat16)


def attend(scalars, queries, flags, blocks, state=None, last=False):
    rows, width = queries.shape
    fresh = state is None
    share = rows // (NY * NXL * NC)
    tile = rows // NC
    count = len(flags)
    state_specs = [
        pl.BlockSpec((HEADS_HERE, tile, 1), lambda i, *_: (0, i, 0)),
        pl.BlockSpec((HEADS_HERE, tile, 2 * HD), lambda i, *_: (0, i, 0)),
    ]
    in_specs = [pl.BlockSpec((NY * NXL * NC, share, width), lambda i, *_: (0, 0, 0))]
    in_specs += [pl.BlockSpec(block.shape, lambda i, *_, rank=block.ndim: (0,) * rank) for block in blocks]
    operands = [queries.reshape(NY * NXL * NC, share, width), *blocks]
    if not fresh:
        in_specs += state_specs
        operands += state
    scratch = [pltpu.VMEM((2, tile, rows), jnp.bfloat16), pltpu.VMEM((2, tile, rows), jnp.float32)]
    if last:
        out_shape = jax.ShapeDtypeStruct((rows, width), jnp.bfloat16)
        out_specs = pl.BlockSpec((tile, width), lambda i, *_: (i, 0))
        scratch = [
            pltpu.VMEM((HEADS_HERE, tile, 2 * HD), jnp.float32),
            pltpu.VMEM((HEADS_HERE, tile, 1), jnp.float32),
            pltpu.VMEM((rows, width), jnp.bfloat16),
            pltpu.VMEM((rows, width), jnp.bfloat16),
        ] + scratch
    else:
        out_shape = [
            jax.ShapeDtypeStruct((HEADS_HERE, rows, 1), jnp.float32),
            jax.ShapeDtypeStruct((HEADS_HERE, rows, 2 * HD), jnp.float32),
        ]
        out_specs = state_specs
    return pl.pallas_call(
        functools.partial(attend_body, fresh, last, flags),
        out_shape=out_shape,
        grid_spec=pltpu.PrefetchScalarGridSpec(
            num_scalar_prefetch=1, grid=(NC,), in_specs=in_specs, out_specs=out_specs, scratch_shapes=scratch
        ),
        compiler_params=pltpu.CompilerParams(vmem_limit_bytes=40 * 1024 * 1024),
        cost_estimate=pl.CostEstimate(
            flops=4 * count * rows * rows * width, bytes_accessed=20 * rows * width, transcendentals=3 * count * rows * rows
        ),
    )(scalars, *operands)


def fetch(keys, values, root, z, xh, scalars, first_pass):
    rows, width = keys.shape
    cut = rows // NZ
    own = jnp.stack([keys.reshape(NZ, cut, width), values.reshape(NZ, cut, width)], axis=1)
    distance = lax.rem(z - root // NXH + NZ, NZ)
    at_root = distance == 0
    lag2_keys = shift(keys, "z", NZ, 1)
    down = shift(own[UP + 1], "z", NZ, -1)
    for number in range(UP + 2, NZ):
        if number == UP + 3:
            down, scalars = lax.optimization_barrier((down, scalars))
        if number == UP + 4:
            down, lag2_keys = lax.optimization_barrier((down, lag2_keys))
        down = shift(jnp.where(at_root, own[number], down), "z", NZ, -1)
    lag1_keys = lax.ppermute(jnp.where(xh == 0, keys, lag2_keys), "xh", SWAP)
    up, lag2_keys = lax.optimization_barrier((own[UP], lag2_keys))
    for number in range(UP, 0, -1):
        up = shift(jnp.where(at_root, own[number], up) if number < UP else up, "z", NZ, 1)
    values_late, up = lax.optimization_barrier((values, up))
    lag2_values = shift(values_late, "z", NZ, 1)
    piece = jnp.where(at_root, own[0], jnp.where(distance <= UP, up, down))
    piece, lag1_keys = lax.optimization_barrier((piece, lag1_keys))
    piece = jnp.where(xh == lax.rem(root, NXH), piece, lax.ppermute(piece, "xh", SWAP))
    piece, lag2_values = lax.optimization_barrier((piece, lag2_values))
    lag1_values = lax.ppermute(jnp.where(xh == 0, values, lag2_values), "xh", SWAP)
    peak, total = first_pass(scalars, [lag2_keys, lag2_values])
    pieces = [piece]
    up = down = piece
    for number in range(4):
        if number == 1:
            up, peak = lax.optimization_barrier((up, peak))
        if number == 2:
            up, lag1_values = lax.optimization_barrier((up, lag1_values))
        up = shift(up, "z", NZ, 1)
        pieces.append(up)
        if number < 3:
            down = shift(down, "z", NZ, -1)
            pieces.append(down)
    return [peak, total], [lag1_keys, lag1_values], pieces, scalars


def add(*terms):
    total = terms[0].astype(jnp.float32)
    for term in terms[1:]:
        total = total + term.astype(jnp.float32)
    return total


def sum_over_y(terms):
    half = terms[0].shape[-1] // 2
    from_below = shift(terms[2][..., :half], "y", NY, 1)
    from_above = shift(terms[2][..., half:], "y", NY, -1)
    rise = jnp.concatenate([add(terms[1][..., :half], from_below).astype(jnp.bfloat16), terms[1][..., half:]], axis=-1)
    fall = jnp.concatenate([terms[3][..., :half], add(terms[3][..., half:], from_above).astype(jnp.bfloat16)], axis=-1)
    return [terms[0], shift(rise, "y", NY, 1), shift(fall, "y", NY, -1)]


def local(queries, keys, values, residual, out_weight, gate_table, noise_steps, windows):
    z, xh, y, xl, core = (lax.axis_index(name) for name in ("z", "xh", "y", "xl", "c"))
    my_span = z * NXH + xh
    span_ids = lax.iota(jnp.int32, NZ * NXH)
    clean_root = jnp.sum(span_ids * (noise_steps == 0).astype(jnp.int32))
    rows, width = queries.shape
    share = residual.shape[0]

    weight = jnp.concatenate([out_weight, lax.ppermute(out_weight, "c", SWAP)], axis=0)
    scalars = jnp.stack(
        [
            jnp.int32(1),
            windows[my_span, 1],
            windows[my_span, 0],
            (my_span != clean_root).astype(jnp.int32),
            y,
            xl,
            core,
        ]
    )

    def first_pass(scalars, lag2):
        return attend(scalars, queries, (0, 1), [keys, values, *lag2])

    state, lag1, pieces, scalars = fetch(keys, values, clean_root, z, xh, scalars, first_pass)
    state = attend(scalars, queries, (2,), lag1, state)
    state, weight = lax.optimization_barrier((state, weight))
    attended = attend(scalars, queries, (3,), pieces, state, last=True)
    taken = lax.ppermute(attended[rows // 2 :], "c", SWAP)
    both = jnp.concatenate([attended[: rows // 2], taken], axis=1)

    def project(low, high):
        terms = jnp.dot(both, weight[:, low:high], preferred_element_type=jnp.float32).astype(jnp.bfloat16)
        return terms.reshape(NXL, NY, share, high - low)

    x_first = project(0, X_FIRST)
    y_first = project(X_FIRST, out_weight.shape[1])

    x_got = lax.ppermute(x_first[1], "xl", SWAP)
    here = sum_over_y([y_first[:, number] for number in range(NY)])
    here_kept = [term[0] for term in here]
    here_sent = add(*[term[1] for term in here]).astype(jnp.bfloat16)
    here_got = lax.ppermute(here_sent, "xl", SWAP)
    x_sum = add(x_first[0], x_got).astype(jnp.bfloat16)
    left = add(x_sum[0], *[shift(x_sum[step], "y", NY, step) for step in (1, 3, 2)])
    right = add(*here_kept, here_got)
    gate_row = lax.dynamic_slice_in_dim(gate_table, noise_steps[my_span], 1, 0)
    summed = jnp.concatenate([left, right], axis=1)
    return (residual.astype(jnp.float32) + gate_row * summed).astype(jnp.bfloat16)


def solution(mesh):
    fine = Mesh(mesh.devices.reshape(NZ, NXH, NY, NXL, NC), ("z", "xh", "y", "xl", "c"))
    span, mp = ("z", "xh"), ("y", "xl", "c")
    in_specs = (
        P(span, mp),
        P(span, mp),
        P(span, mp),
        P(span + mp, None),
        P(mp, None),
        P(),
        P(),
        P(),
    )
    out_specs = P(span + mp, None)
    return jax.shard_map(local, mesh=fine, in_specs=in_specs, out_specs=out_specs, check_vma=False)
```

profile of v0, /device:TPU:28, one launch (start us, length us, event | category | flops | bytes accessed | tf_op | source)
XLA Modules:
  0.0 152.3 jit_solution(1011462352895045122)
XLA Ops:
  1.3 5.9 %collective-permute-start = (bf16[2,96,384]{2,1,0:T(8,128)(2,1)S(1)}, bf16[2,96,384]{2,1,0:T(8,128)(2,1)S(1)}, u32[]{:S(2)}, u32[]{:S(2)}) collective-permute-start(bf16[2,96,384]{2,1,0:T(8,128)(2,1)S(1)} %get-tuple-element.59), channel_id=1, source_target_pairs={{0,224},{32,0},{64,32},{96,64},{128,96},{160,128},{192,160},{224,1... | collective-permute-start | bytes 442376 | tf_op jit(solution)/shard_map/ppermute | solution.py:22
  10.9 3.8 %collective-permute-start.1 = (bf16[2,96,384]{2,1,0:T(8,128)(2,1)S(1)}, bf16[2,96,384]{2,1,0:T(8,128)(2,1)S(1)}, u32[]{:S(2)}, u32[]{:S(2)}) collective-permute-start(bf16[2,96,384]{2,1,0:T(8,128)(2,1)S(1)} %bitcast_select_fusion.4), channel_id=1, source_target_pairs={{0,224},{32,0},{64,32},{96,64},{128,96},{160,128},{192,160},{224,1... | collective-permute-start | bytes 442376 | tf_op jit(solution)/shard_map/ppermute | solution.py:22
  17.6 3.8 %collective-permute-start.2 = (bf16[2,96,384]{2,1,0:T(8,128)(2,1)S(1)}, bf16[2,96,384]{2,1,0:T(8,128)(2,1)S(1)}, u32[]{:S(2)}, u32[]{:S(2)}) collective-permute-start(bf16[2,96,384]{2,1,0:T(8,128)(2,1)S(1)} %bitcast_select_fusion.1), channel_id=1, source_target_pairs={{0,224},{32,0},{64,32},{96,64},{128,96},{160,128},{192,160},{224,1... | collective-permute-start | bytes 442376 | tf_op jit(solution)/shard_map/ppermute | solution.py:22
  21.4 2.7 %collective-permute-done.2 = bf16[2,96,384]{2,1,0:T(8,128)(2,1)S(1)} collective-permute-done((bf16[2,96,384]{2,1,0:T(8,128)(2,1)S(1)}, bf16[2,96,384]{2,1,0:T(8,128)(2,1)S(1)}, u32[]{:S(2)}, u32[]{:S(2)}) %collective-permute-start.2) | collective-permute-done | bytes 147488 | tf_op jit(solution)/shard_map/ppermute | solution.py:22
  24.1 3.8 %collective-permute-start.6 = (bf16[2,96,384]{2,1,0:T(8,128)(2,1)S(1)}, bf16[2,96,384]{2,1,0:T(8,128)(2,1)S(1)}, u32[]{:S(2)}, u32[]{:S(2)}) collective-permute-start(bf16[2,96,384]{2,1,0:T(8,128)(2,1)S(1)} %fusion.17), channel_id=1, source_target_pairs={{0,224},{32,0},{64,32},{96,64},{128,96},{160,128},{192,160},{224,1... | collective-permute-start | bytes 442376 | tf_op jit(solution)/shard_map/ppermute | solution.py:22
  31.3 3.1 %collective-permute-start.7 = (bf16[2,96,384]{2,1,0:T(8,128)(2,1)S(1)}, bf16[2,96,384]{2,1,0:T(8,128)(2,1)S(1)}, u32[]{:S(2)}, u32[]{:S(2)}) collective-permute-start(bf16[2,96,384]{2,1,0:T(8,128)(2,1)S(1)} %get-tuple-element.56), channel_id=1, source_target_pairs={{0,224},{32,0},{64,32},{96,64},{128,96},{160,128},{192,160},{224,1... | collective-permute-start | bytes 442376 | tf_op jit(solution)/shard_map/ppermute | solution.py:22
  34.5 3.0 %collective-permute-done.5 = bf16[2,96,384]{2,1,0:T(8,128)(2,1)S(1)} collective-permute-done((bf16[2,96,384]{2,1,0:T(8,128)(2,1)S(1)}, bf16[2,96,384]{2,1,0:T(8,128)(2,1)S(1)}, u32[]{:S(2)}, u32[]{:S(2)}) %collective-permute-start.5) | collective-permute-done | bytes 147488 | tf_op jit(solution)/shard_map/ppermute | solution.py:22
  37.7 6.1 %collective-permute-done.8.refs_2_ = bf16[768,384]{1,0:T(8,128)(2,1)S(1)} collective-permute-done((bf16[768,384]{1,0:T(8,128)(2,1)}, bf16[768,384]{1,0:T(8,128)(2,1)S(1)}, u32[]{:S(2)}, u32[]{:S(2)}) %collective-permute-start.8) | collective-permute-done | bytes 589856 | tf_op jit(solution)/shard_map/ppermute | solution.py:160
  44.2 6.2 %collective-permute-done.9 = bf16[2,96,384]{2,1,0:T(8,128)(2,1)} collective-permute-done((bf16[2,96,384]{2,1,0:T(8,128)(2,1)S(1)}, bf16[2,96,384]{2,1,0:T(8,128)(2,1)}, u32[]{:S(2)}, u32[]{:S(2)}) %collective-permute-start.9) | collective-permute-done | bytes 147488 | tf_op jit(solution)/shard_map/ppermute | solution.py:168
  52.3 3.2 %collective-permute-start.12 = (bf16[2,96,384]{2,1,0:T(8,128)(2,1)S(1)}, bf16[2,96,384]{2,1,0:T(8,128)(2,1)}, u32[]{:S(2)}, u32[]{:S(2)}) collective-permute-start(bf16[2,96,384]{2,1,0:T(8,128)(2,1)S(1)} %broadcast_select_fusion.2.refs_2_), channel_id=1, source_target_pairs={{0,224},{32,0},{64,32},{96,64},{128,96},{160,128},{192,160},{224,1... | collective-permute-start | bytes 442376 | tf_op jit(solution)/shard_map/ppermute | solution.py:22
  57.7 7.3 %shard_map.82 = (f32[3,768,1]{2,1,0:T(8,128)S(1)}, f32[3,768,256]{2,1,0:T(8,128)S(1)}) custom-call(s32[7]{0:T(128)S(1)} %stack.27.refs_0_, bf16[16,48,384]{2,1,0:T(8,128)(2,1)S(1)} %bitcast.96, bf16[768,384]{1,0:T(8,128)(2,1)S(1)} %copy-done.2, bf16[768,384]{1,0:T(8,128)(2,1)S(1)} %copy-done.1, bf16[768,384]{1,0:T(8,128)(2,1)S(1)} %copy-done.7, ...), custom_call_target="tpu_custom_call" | custom-call | flops 1811939328 | bytes 5898240 | tf_op jit(solution)/shard_map/pallas_call | solution.py:133
  67.0 3.2 %collective-permute-start.14 = (bf16[2,96,384]{2,1,0:T(8,128)(2,1)}, bf16[2,96,384]{2,1,0:T(8,128)(2,1)}, u32[]{:S(2)}, u32[]{:S(2)}) collective-permute-start(bf16[2,96,384]{2,1,0:T(8,128)(2,1)} %collective-permute-done.12.refs_4_), channel_id=1, source_target_pairs={{0,224},{32,0},{64,32},{96,64},{128,96},{160,128},{192,160},{224,1... | collective-permute-start | bytes 442376 | tf_op jit(solution)/shard_map/ppermute | solution.py:22
  70.3 3.7 %collective-permute-done.13.refs_5_ = bf16[2,96,384]{2,1,0:T(8,128)(2,1)} collective-permute-done((bf16[2,96,384]{2,1,0:T(8,128)(2,1)S(1)}, bf16[2,96,384]{2,1,0:T(8,128)(2,1)}, u32[]{:S(2)}, u32[]{:S(2)}) %collective-permute-start.13) | collective-permute-done | bytes 147488 | tf_op jit(solution)/shard_map/ppermute | solution.py:22
  77.4 3.3 %collective-permute-start.17 = (bf16[2,96,384]{2,1,0:T(8,128)(2,1)}, bf16[2,96,384]{2,1,0:T(8,128)(2,1)S(1)}, u32[]{:S(2)}, u32[]{:S(2)}) collective-permute-start(bf16[2,96,384]{2,1,0:T(8,128)(2,1)} %collective-permute-done.14.refs_6_), channel_id=1, source_target_pairs={{0,224},{32,0},{64,32},{96,64},{128,96},{160,128},{192,160},{224,1... | collective-permute-start | bytes 442376 | tf_op jit(solution)/shard_map/ppermute | solution.py:22
  84.5 4.8 %shard_map.83 = (f32[3,768,1]{2,1,0:T(8,128)S(1)}, f32[3,768,256]{2,1,0:T(8,128)S(1)}) custom-call(s32[7]{0:T(128)S(1)} %stack.27.refs_0_, bf16[16,48,384]{2,1,0:T(8,128)(2,1)S(1)} %bitcast.97, bf16[768,384]{1,0:T(8,128)(2,1)S(1)} %copy-done.9, bf16[768,384]{1,0:T(8,128)(2,1)S(1)} %copy-done.11, f32[3,768,1]{2,1,0:T(8,128)S(1)} %get-tuple-element.44.refs_4_, ...), custom_call_target="tpu_custom_call" | custom-call | flops 905969664 | bytes 5898240 | tf_op jit(solution)/shard_map/pallas_call | solution.py:133
  89.5 3.7 %pad_maximum_fusion = bf16[768,6144]{1,0:T(8,128)(2,1)S(1)} fusion(bf16[384,6144]{1,0:T(8,128)(2,1)} %collective-permute-done.19, bf16[384,6144]{1,0:T(8,128)(2,1)S(1)} %copy-done.16), kind=kLoop, calls=%fused_computation | loop fusion | flops 18874368 | bytes 18874368 | tf_op jit(solution)/shard_map/concatenate | solution.py:211
  93.2 2.8 %collective-permute-done.18.refs_9_ = bf16[2,96,384]{2,1,0:T(8,128)(2,1)S(1)} collective-permute-done((bf16[2,96,384]{2,1,0:T(8,128)(2,1)}, bf16[2,96,384]{2,1,0:T(8,128)(2,1)S(1)}, u32[]{:S(2)}, u32[]{:S(2)}) %collective-permute-start.18) | collective-permute-done | bytes 147488 | tf_op jit(solution)/shard_map/ppermute | solution.py:22
  96.0 6.0 %shard_map.84 = bf16[768,384]{1,0:T(8,128)(2,1)S(1)} custom-call(s32[7]{0:T(128)S(1)} %stack.27.refs_0_, bf16[16,48,384]{2,1,0:T(8,128)(2,1)S(1)} %bitcast.98, bf16[2,96,384]{2,1,0:T(8,128)(2,1)S(1)} %broadcast_select_fusion.2.refs_2_, bf16[2,96,384]{2,1,0:T(8,128)(2,1)S(1)} %copy-done.15, bf16[2,96,384]{2,1,0:T(8,128)(2,1)} %collective-permute-done.12.refs_4_, ...), custom_call_target="tpu_custom_call" | custom-call | flops 905969664 | bytes 5898240 | tf_op jit(solution)/shard_map/pallas_call | solution.py:133
  112.9 3.9 %collective-permute-done.25 = bf16[2,48,1728]{2,1,0:T(8,128)(2,1)S(1)} collective-permute-done((bf16[2,48,1728]{2,1,0:T(8,128)(2,1)S(1)}, bf16[2,48,1728]{2,1,0:T(8,128)(2,1)S(1)}, u32[]{:S(2)}, u32[]{:S(2)}) %collective-permute-start.25) | collective-permute-done | bytes 331808 | tf_op jit(solution)/shard_map/ppermute | solution.py:22
  118.6 3.3 %collective-permute-done.27 = bf16[2,48,1728]{2,1,0:T(8,128)(2,1)S(1)} collective-permute-done((bf16[2,48,1728]{2,1,0:T(8,128)(2,1)S(1)}, bf16[2,48,1728]{2,1,0:T(8,128)(2,1)S(1)}, u32[]{:S(2)}, u32[]{:S(2)}) %collective-permute-start.27) | collective-permute-done | bytes 331808 | tf_op jit(solution)/shard_map/ppermute | solution.py:22
  122.8 10.9 %collective-permute-done.21 = bf16[4,48,2688]{2,1,0:T(8,128)(2,1)S(1)} collective-permute-done((bf16[4,48,2688]{2,1,0:T(8,128)(2,1)S(1)}, bf16[4,48,2688]{2,1,0:T(8,128)(2,1)S(1)}, u32[]{:S(2)}, u32[]{:S(2)}) %collective-permute-start.21) | collective-permute-done | bytes 1032224 | tf_op jit(solution)/shard_map/ppermute | solution.py:241
  136.2 2.5 %collective-permute-start.24 = (bf16[48,2688]{1,0:T(8,128)(2,1)S(1)}, bf16[48,2688]{1,0:T(8,128)(2,1)S(1)}, u32[]{:S(2)}, u32[]{:S(2)}) collective-permute-start(bf16[48,2688]{1,0:T(8,128)(2,1)S(1)} %get-tuple-element.61), channel_id=1, source_target_pairs={{0,8},{4,12},{8,0},{12,4},{1,9},{5,13},{9,1},{13,5},{2,10},{6,14},... | collective-permute-start | bytes 774152 | tf_op jit(solution)/shard_map/ppermute | solution.py:22
  140.7 2.6 %collective-permute-done.22 = bf16[48,2688]{1,0:T(8,128)(2,1)S(1)} collective-permute-done((bf16[48,2688]{1,0:T(8,128)(2,1)S(1)}, bf16[48,2688]{1,0:T(8,128)(2,1)S(1)}, u32[]{:S(2)}, u32[]{:S(2)}) %collective-permute-start.22) | collective-permute-done | bytes 258080 | tf_op jit(solution)/shard_map/ppermute | solution.py:22
  143.3 6.9 %collective-permute-done.23 = bf16[48,2688]{1,0:T(8,128)(2,1)S(1)} collective-permute-done((bf16[48,2688]{1,0:T(8,128)(2,1)S(1)}, bf16[48,2688]{1,0:T(8,128)(2,1)S(1)}, u32[]{:S(2)}, u32[]{:S(2)}) %collective-permute-start.23) | collective-permute-done | bytes 258080 | tf_op jit(solution)/shard_map/ppermute | solution.py:22
  (114 shorter events, 40.3 us)
Async XLA Ops:
  0.0 89.4 %collective-permute-start.19 = (bf16[384,6144]{1,0:T(8,128)(2,1)}, bf16[384,6144]{1,0:T(8,128)(2,1)}, u32[]{:S(2)}, u32[]{:S(2)}) collective-permute-start(bf16[384,6144]{1,0:T(8,128)(2,1)} %param.12), channel_id=1, source_target_pairs={{0,1},{1,0},{2,3},{3,2},{4,5},{5,4},{6,7},{7,6},{8,9},{9,8},{10,11... | collective-permute-start | bytes 14155784 | tf_op jit(solution)/shard_map/ppermute | solution.py:211
  1.3 9.6 %collective-permute-start = (bf16[2,96,384]{2,1,0:T(8,128)(2,1)S(1)}, bf16[2,96,384]{2,1,0:T(8,128)(2,1)S(1)}, u32[]{:S(2)}, u32[]{:S(2)}) collective-permute-start(bf16[2,96,384]{2,1,0:T(8,128)(2,1)S(1)} %get-tuple-element.59), channel_id=1, source_target_pairs={{0,224},{32,0},{64,32},{96,64},{128,96},{160,128},{192,160},{224,1... | collective-permute-start | bytes 442376 | tf_op jit(solution)/shard_map/ppermute | solution.py:22
  7.2 16.9 %collective-permute-start.3 = (bf16[768,384]{1,0:T(8,128)(2,1)S(1)}, bf16[768,384]{1,0:T(8,128)(2,1)S(1)}, u32[]{:S(2)}, u32[]{:S(2)}) collective-permute-start(bf16[768,384]{1,0:T(8,128)(2,1)S(1)} %copy-done.2), channel_id=1, source_target_pairs={{0,32},{32,64},{64,96},{96,128},{128,160},{160,192},{192,224},{224... | collective-permute-start | bytes 1769480 | tf_op jit(solution)/shard_map/ppermute | solution.py:22
  24.1 6.8 %collective-permute-start.4 = (bf16[2,96,384]{2,1,0:T(8,128)(2,1)S(1)}, bf16[2,96,384]{2,1,0:T(8,128)(2,1)S(1)}, u32[]{:S(2)}, u32[]{:S(2)}) collective-permute-start(bf16[2,96,384]{2,1,0:T(8,128)(2,1)S(1)} %get-tuple-element.31), channel_id=1, source_target_pairs={{0,32},{32,64},{64,96},{96,128},{128,160},{160,192},{192,224},{224... | collective-permute-start | bytes 442376 | tf_op jit(solution)/shard_map/ppermute | solution.py:22
  24.1 6.8 %collective-permute-start.6 = (bf16[2,96,384]{2,1,0:T(8,128)(2,1)S(1)}, bf16[2,96,384]{2,1,0:T(8,128)(2,1)S(1)}, u32[]{:S(2)}, u32[]{:S(2)}) collective-permute-start(bf16[2,96,384]{2,1,0:T(8,128)(2,1)S(1)} %fusion.17), channel_id=1, source_target_pairs={{0,224},{32,0},{64,32},{96,64},{128,96},{160,128},{192,160},{224,1... | collective-permute-start | bytes 442376 | tf_op jit(solution)/shard_map/ppermute | solution.py:22
  28.8 15.0 %collective-permute-start.8 = (bf16[768,384]{1,0:T(8,128)(2,1)}, bf16[768,384]{1,0:T(8,128)(2,1)S(1)}, u32[]{:S(2)}, u32[]{:S(2)}) collective-permute-start(bf16[768,384]{1,0:T(8,128)(2,1)} %broadcast_select_fusion.1), channel_id=1, source_target_pairs={{0,16},{16,0},{1,17},{17,1},{2,18},{18,2},{3,19},{19,3},{4,20},{20... | collective-permute-start | bytes 1769480 | tf_op jit(solution)/shard_map/ppermute | solution.py:160
  37.5 13.9 %collective-permute-start.10 = (bf16[768,384]{1,0:T(8,128)(2,1)S(1)}, bf16[768,384]{1,0:T(8,128)(2,1)S(1)}, u32[]{:S(2)}, u32[]{:S(2)}) collective-permute-start(bf16[768,384]{1,0:T(8,128)(2,1)S(1)} %copy-done.1), channel_id=1, source_target_pairs={{0,32},{32,64},{64,96},{96,128},{128,160},{160,192},{192,224},{224... | collective-permute-start | bytes 1769480 | tf_op jit(solution)/shard_map/ppermute | solution.py:22
  43.7 6.8 %collective-permute-start.9 = (bf16[2,96,384]{2,1,0:T(8,128)(2,1)S(1)}, bf16[2,96,384]{2,1,0:T(8,128)(2,1)}, u32[]{:S(2)}, u32[]{:S(2)}) collective-permute-start(bf16[2,96,384]{2,1,0:T(8,128)(2,1)S(1)} %bitcast_select_fusion.3), channel_id=1, source_target_pairs={{0,16},{16,0},{1,17},{17,1},{2,18},{18,2},{3,19},{19,3},{4,20},{20... | collective-permute-start | bytes 442376 | tf_op jit(solution)/shard_map/ppermute | solution.py:168
  51.5 22.4 %collective-permute-start.15 = (bf16[768,384]{1,0:T(8,128)(2,1)S(1)}, bf16[768,384]{1,0:T(8,128)(2,1)S(1)}, u32[]{:S(2)}, u32[]{:S(2)}) collective-permute-start(bf16[768,384]{1,0:T(8,128)(2,1)S(1)} %broadcast_select_fusion), channel_id=1, source_target_pairs={{0,16},{16,0},{1,17},{17,1},{2,18},{18,2},{3,19},{19,3},{4,20},{20... | collective-permute-start | bytes 1769480 | tf_op jit(solution)/shard_map/ppermute | solution.py:170
  52.3 14.1 %collective-permute-start.11 = (bf16[2,96,384]{2,1,0:T(8,128)(2,1)S(1)}, bf16[2,96,384]{2,1,0:T(8,128)(2,1)S(1)}, u32[]{:S(2)}, u32[]{:S(2)}) collective-permute-start(bf16[2,96,384]{2,1,0:T(8,128)(2,1)S(1)} %broadcast_select_fusion.2.refs_2_), channel_id=1, source_target_pairs={{0,32},{32,64},{64,96},{96,128},{128,160},{160,192},{192,224},{224... | collective-permute-start | bytes 442376 | tf_op jit(solution)/shard_map/ppermute | solution.py:22
  52.3 14.7 %collective-permute-start.12 = (bf16[2,96,384]{2,1,0:T(8,128)(2,1)S(1)}, bf16[2,96,384]{2,1,0:T(8,128)(2,1)}, u32[]{:S(2)}, u32[]{:S(2)}) collective-permute-start(bf16[2,96,384]{2,1,0:T(8,128)(2,1)S(1)} %broadcast_select_fusion.2.refs_2_), channel_id=1, source_target_pairs={{0,224},{32,0},{64,32},{96,64},{128,96},{160,128},{192,160},{224,1... | collective-permute-start | bytes 442376 | tf_op jit(solution)/shard_map/ppermute | solution.py:22
  66.4 7.6 %collective-permute-start.13 = (bf16[2,96,384]{2,1,0:T(8,128)(2,1)S(1)}, bf16[2,96,384]{2,1,0:T(8,128)(2,1)}, u32[]{:S(2)}, u32[]{:S(2)}) collective-permute-start(bf16[2,96,384]{2,1,0:T(8,128)(2,1)S(1)} %collective-permute-done.11.refs_3_), channel_id=1, source_target_pairs={{0,32},{32,64},{64,96},{96,128},{128,160},{160,192},{192,224},{224... | collective-permute-start | bytes 442376 | tf_op jit(solution)/shard_map/ppermute | solution.py:22
  67.0 10.3 %collective-permute-start.14 = (bf16[2,96,384]{2,1,0:T(8,128)(2,1)}, bf16[2,96,384]{2,1,0:T(8,128)(2,1)}, u32[]{:S(2)}, u32[]{:S(2)}) collective-permute-start(bf16[2,96,384]{2,1,0:T(8,128)(2,1)} %collective-permute-done.12.refs_4_), channel_id=1, source_target_pairs={{0,224},{32,0},{64,32},{96,64},{128,96},{160,128},{192,160},{224,1... | collective-permute-start | bytes 442376 | tf_op jit(solution)/shard_map/ppermute | solution.py:22
  74.8 14.5 %collective-permute-start.16 = (bf16[2,96,384]{2,1,0:T(8,128)(2,1)}, bf16[2,96,384]{2,1,0:T(8,128)(2,1)}, u32[]{:S(2)}, u32[]{:S(2)}) collective-permute-start(bf16[2,96,384]{2,1,0:T(8,128)(2,1)} %collective-permute-done.13.refs_5_), channel_id=1, source_target_pairs={{0,32},{32,64},{64,96},{96,128},{128,160},{160,192},{192,224},{224... | collective-permute-start | bytes 442376 | tf_op jit(solution)/shard_map/ppermute | solution.py:22
  77.4 15.8 %collective-permute-start.17 = (bf16[2,96,384]{2,1,0:T(8,128)(2,1)}, bf16[2,96,384]{2,1,0:T(8,128)(2,1)S(1)}, u32[]{:S(2)}, u32[]{:S(2)}) collective-permute-start(bf16[2,96,384]{2,1,0:T(8,128)(2,1)} %collective-permute-done.14.refs_6_), channel_id=1, source_target_pairs={{0,224},{32,0},{64,32},{96,64},{128,96},{160,128},{192,160},{224,1... | collective-permute-start | bytes 442376 | tf_op jit(solution)/shard_map/ppermute | solution.py:22
  106.6 10.2 %collective-permute-start.25 = (bf16[2,48,1728]{2,1,0:T(8,128)(2,1)S(1)}, bf16[2,48,1728]{2,1,0:T(8,128)(2,1)S(1)}, u32[]{:S(2)}, u32[]{:S(2)}) collective-permute-start(bf16[2,48,1728]{2,1,0:T(8,128)(2,1)S(1)} %get-tuple-element.63), channel_id=1, source_target_pairs={{0,4},{4,8},{8,12},{12,0},{1,5},{5,9},{9,13},{13,1},{2,6},{6,10},{... | collective-permute-start | bytes 995336 | tf_op jit(solution)/shard_map/ppermute | solution.py:22
  109.0 24.7 %collective-permute-start.21 = (bf16[4,48,2688]{2,1,0:T(8,128)(2,1)S(1)}, bf16[4,48,2688]{2,1,0:T(8,128)(2,1)S(1)}, u32[]{:S(2)}, u32[]{:S(2)}) collective-permute-start(bf16[4,48,2688]{2,1,0:T(8,128)(2,1)S(1)} %bitcast.103), channel_id=1, source_target_pairs={{0,2},{2,0},{1,3},{3,1},{4,6},{6,4},{5,7},{7,5},{8,10},{10,8},{9,1... | collective-permute-start | bytes 3096584 | tf_op jit(solution)/shard_map/ppermute | solution.py:241
  111.0 10.9 %collective-permute-start.27 = (bf16[2,48,1728]{2,1,0:T(8,128)(2,1)S(1)}, bf16[2,48,1728]{2,1,0:T(8,128)(2,1)S(1)}, u32[]{:S(2)}, u32[]{:S(2)}) collective-permute-start(bf16[2,48,1728]{2,1,0:T(8,128)(2,1)S(1)} %get-tuple-element.64), channel_id=1, source_target_pairs={{0,12},{4,0},{8,4},{12,8},{1,13},{5,1},{9,5},{13,9},{2,14},{6,2},{... | collective-permute-start | bytes 995336 | tf_op jit(solution)/shard_map/ppermute | solution.py:22
  117.1 21.6 %collective-permute-start.26 = (bf16[2,48,3456]{2,1,0:T(8,128)(2,1)S(1)}, bf16[2,48,3456]{2,1,0:T(8,128)(2,1)S(1)}, u32[]{:S(2)}, u32[]{:S(2)}) collective-permute-start(bf16[2,48,3456]{2,1,0:T(8,128)(2,1)S(1)} %pad_maximum_fusion.1), channel_id=1, source_target_pairs={{0,4},{4,8},{8,12},{12,0},{1,5},{5,9},{9,13},{13,1},{2,6},{6,10},{... | collective-permute-start | bytes 1990664 | tf_op jit(solution)/shard_map/ppermute | solution.py:22
  122.2 17.7 %collective-permute-start.28 = (bf16[2,48,3456]{2,1,0:T(8,128)(2,1)S(1)}, bf16[2,48,3456]{2,1,0:T(8,128)(2,1)S(1)}, u32[]{:S(2)}, u32[]{:S(2)}) collective-permute-start(bf16[2,48,3456]{2,1,0:T(8,128)(2,1)S(1)} %pad_maximum_fusion.2), channel_id=1, source_target_pairs={{0,12},{4,0},{8,4},{12,8},{1,13},{5,1},{9,5},{13,9},{2,14},{6,2},{... | collective-permute-start | bytes 1990664 | tf_op jit(solution)/shard_map/ppermute | solution.py:22
  134.1 9.2 %collective-permute-start.22 = (bf16[48,2688]{1,0:T(8,128)(2,1)S(1)}, bf16[48,2688]{1,0:T(8,128)(2,1)S(1)}, u32[]{:S(2)}, u32[]{:S(2)}) collective-permute-start(bf16[48,2688]{1,0:T(8,128)(2,1)S(1)} %get-tuple-element.60), channel_id=1, source_target_pairs={{0,4},{4,8},{8,12},{12,0},{1,5},{5,9},{9,13},{13,1},{2,6},{6,10},{... | collective-permute-start | bytes 774152 | tf_op jit(solution)/shard_map/ppermute | solution.py:22
  135.6 14.5 %collective-permute-start.23 = (bf16[48,2688]{1,0:T(8,128)(2,1)S(1)}, bf16[48,2688]{1,0:T(8,128)(2,1)S(1)}, u32[]{:S(2)}, u32[]{:S(2)}) collective-permute-start(bf16[48,2688]{1,0:T(8,128)(2,1)S(1)} %get-tuple-element.62), channel_id=1, source_target_pairs={{0,12},{4,0},{8,4},{12,8},{1,13},{5,1},{9,5},{13,9},{2,14},{6,2},{... | collective-permute-start | bytes 774152 | tf_op jit(solution)/shard_map/ppermute | solution.py:22
  136.2 14.0 %collective-permute-start.24 = (bf16[48,2688]{1,0:T(8,128)(2,1)S(1)}, bf16[48,2688]{1,0:T(8,128)(2,1)S(1)}, u32[]{:S(2)}, u32[]{:S(2)}) collective-permute-start(bf16[48,2688]{1,0:T(8,128)(2,1)S(1)} %get-tuple-element.61), channel_id=1, source_target_pairs={{0,8},{4,12},{8,0},{12,4},{1,9},{5,13},{9,1},{13,5},{2,10},{6,14},... | collective-permute-start | bytes 774152 | tf_op jit(solution)/shard_map/ppermute | solution.py:22
  140.1 10.2 %collective-permute-start.29 = (bf16[48,3456]{1,0:T(8,128)(2,1)S(1)}, bf16[48,3456]{1,0:T(8,128)(2,1)S(1)}, u32[]{:S(2)}, u32[]{:S(2)}) collective-permute-start(bf16[48,3456]{1,0:T(8,128)(2,1)S(1)} %fusion.5), channel_id=1, source_target_pairs={{0,2},{2,0},{1,3},{3,1},{4,6},{6,4},{5,7},{7,5},{8,10},{10,8},{9,1... | collective-permute-start | bytes 995336 | tf_op jit(solution)/shard_map/ppermute | solution.py:245
  (27 other events, 244.0 us)
where the time goes:
time: 151 us; the launch traced here: 152 us
  waiting for transfers between devices  57.3 us (38%)
  starting transfers between devices  44.3 us (29%)
  Pallas kernels  18.1 us (12%)
  local copies, waits for them, and re-layouts  13.1 us (9%)
  other arithmetic  9.8 us (6%)
  between operations  5.56 us (4%)
  matrix products  4.3 us (3%)
    ppermute x23, starting transfers between devices, shift(): lax.ppermute(value, axis, [(i, (i + steps) % count) for i in range(count)])  39.7 us
    ppermute x23, waiting for transfers between devices, shift(): lax.ppermute(value, axis, [(i, (i + steps) % count) for i in range(count)])  32.5 us
    pallas_call x3, Pallas kernels, attend(): pl.pallas_call(functools.partial(attend_body, fresh, last, flags), out_sh...  18.1 us
    ppermute x1, waiting for transfers between devices, local(): x_got = lax.ppermute(x_first[1], 'xl', SWAP)  10.9 us
    unnamed x42, local copies, waits for them, and re-layouts  9.75 us
    ppermute x1, waiting for transfers between devices, fetch(): lax.ppermute(piece, 'xh', SWAP)  6.24 us
    ppermute x1, waiting for transfers between devices, fetch(): lag1_keys = lax.ppermute(jnp.where(xh == 0, keys, lag2_keys), 'xh', SWAP)  6.07 us
    dot_general x2, matrix products, project(): jnp.dot(both, weight[:, low:high], preferred_element_type=jnp.float32)  4.3 us
  transfers between devices with their start and end apart: 30, of which 16 were waited for; matrix products, arithmetic and copies ran while one was open for 9% of the time, Pallas kernels for 8%

commit v1 on v0

--- a/solution.py
+++ b/solution.py
@@ -136,7 +136,7 @@
         grid_spec=pltpu.PrefetchScalarGridSpec(
             num_scalar_prefetch=1, grid=(NC,), in_specs=in_specs, out_specs=out_specs, scratch_shapes=scratch
         ),
-        compiler_params=pltpu.CompilerParams(vmem_limit_bytes=40 * 1024 * 1024),
+        compiler_params=pltpu.CompilerParams(vmem_limit_bytes=20 * 1024 * 1024),
         cost_estimate=pl.CostEstimate(
             flops=4 * count * rows * rows * width, bytes_accessed=20 * rows * width, transcendentals=3 * count * rows * rows
         ),

time: 151 us -> 154 us (1.020)
  the two profiles are of different devices: /device:TPU:28 before, /device:TPU:24 now
where the time goes in v1:
time: 154 us
  waiting for transfers between devices  52.2 us (34%)
  starting transfers between devices  50.8 us (33%)
  Pallas kernels  18.1 us (12%)
  local copies, waits for them, and re-layouts  13.1 us (9%)
  other arithmetic  9.64 us (6%)
  between operations  5.56 us (4%)
  matrix products  4.25 us (3%)
    ppermute x23, starting transfers between devices, shift(): lax.ppermute(value, axis, [(i, (i + steps) % count) for i in range(count)])  39.4 us
    ppermute x23, waiting for transfers between devices, shift(): lax.ppermute(value, axis, [(i, (i + steps) % count) for i in range(count)])  29.6 us
    pallas_call x3, Pallas kernels, attend(): pl.pallas_call(functools.partial(attend_body, fresh, last, flags), out_sh...  18.1 us
    ppermute x1, waiting for transfers between devices, local(): x_got = lax.ppermute(x_first[1], 'xl', SWAP)  11.9 us
    unnamed x42, local copies, waits for them, and re-layouts  9.75 us
    ppermute x1, waiting for transfers between devices, fetch(): lag1_keys = lax.ppermute(jnp.where(xh == 0, keys, lag2_keys), 'xh', SWAP)  5.39 us
    dot_general x2, matrix products, project(): jnp.dot(both, weight[:, low:high], preferred_element_type=jnp.float32)  4.25 us
    ppermute x1, waiting for transfers between devices, fetch(): lax.ppermute(piece, 'xh', SWAP)  3.73 us
  transfers between devices with their start and end apart: 30, of which 15 were waited for; matrix products, arithmetic and copies ran while one was open for 9% of the time, Pallas kernels for 8%

profile of v1, /device:TPU:24, one launch (start us, length us, event | category | flops | bytes accessed | tf_op | source)
XLA Modules:
  0.0 153.6 jit_solution(7562324094304393631)
XLA Ops:
  1.3 5.9 %collective-permute-start = (bf16[2,96,384]{2,1,0:T(8,128)(2,1)S(1)}, bf16[2,96,384]{2,1,0:T(8,128)(2,1)S(1)}, u32[]{:S(2)}, u32[]{:S(2)}) collective-permute-start(bf16[2,96,384]{2,1,0:T(8,128)(2,1)S(1)} %get-tuple-element.59), channel_id=1, source_target_pairs={{0,224},{32,0},{64,32},{96,64},{128,96},{160,128},{192,160},{224,1... | collective-permute-start | bytes 442376 | tf_op jit(solution)/shard_map/ppermute | solution.py:22
  10.9 3.8 %collective-permute-start.1 = (bf16[2,96,384]{2,1,0:T(8,128)(2,1)S(1)}, bf16[2,96,384]{2,1,0:T(8,128)(2,1)S(1)}, u32[]{:S(2)}, u32[]{:S(2)}) collective-permute-start(bf16[2,96,384]{2,1,0:T(8,128)(2,1)S(1)} %bitcast_select_fusion.4), channel_id=1, source_target_pairs={{0,224},{32,0},{64,32},{96,64},{128,96},{160,128},{192,160},{224,1... | collective-permute-start | bytes 442376 | tf_op jit(solution)/shard_map/ppermute | solution.py:22
  17.6 3.8 %collective-permute-start.2 = (bf16[2,96,384]{2,1,0:T(8,128)(2,1)S(1)}, bf16[2,96,384]{2,1,0:T(8,128)(2,1)S(1)}, u32[]{:S(2)}, u32[]{:S(2)}) collective-permute-start(bf16[2,96,384]{2,1,0:T(8,128)(2,1)S(1)} %bitcast_select_fusion.1), channel_id=1, source_target_pairs={{0,224},{32,0},{64,32},{96,64},{128,96},{160,128},{192,160},{224,1... | collective-permute-start | bytes 442376 | tf_op jit(solution)/shard_map/ppermute | solution.py:22
  24.1 3.8 %collective-permute-start.6 = (bf16[2,96,384]{2,1,0:T(8,128)(2,1)S(1)}, bf16[2,96,384]{2,1,0:T(8,128)(2,1)S(1)}, u32[]{:S(2)}, u32[]{:S(2)}) collective-permute-start(bf16[2,96,384]{2,1,0:T(8,128)(2,1)S(1)} %fusion.17), channel_id=1, source_target_pairs={{0,224},{32,0},{64,32},{96,64},{128,96},{160,128},{192,160},{224,1... | collective-permute-start | bytes 442376 | tf_op jit(solution)/shard_map/ppermute | solution.py:22
  28.8 3.0 %collective-permute-start.8 = (bf16[768,384]{1,0:T(8,128)(2,1)}, bf16[768,384]{1,0:T(8,128)(2,1)S(1)}, u32[]{:S(2)}, u32[]{:S(2)}) collective-permute-start(bf16[768,384]{1,0:T(8,128)(2,1)} %broadcast_select_fusion.1), channel_id=1, source_target_pairs={{0,16},{16,0},{1,17},{17,1},{2,18},{18,2},{3,19},{19,3},{4,20},{20... | collective-permute-start | bytes 1769480 | tf_op jit(solution)/shard_map/ppermute | solution.py:160
  31.9 3.2 %collective-permute-start.7 = (bf16[2,96,384]{2,1,0:T(8,128)(2,1)S(1)}, bf16[2,96,384]{2,1,0:T(8,128)(2,1)S(1)}, u32[]{:S(2)}, u32[]{:S(2)}) collective-permute-start(bf16[2,96,384]{2,1,0:T(8,128)(2,1)S(1)} %get-tuple-element.56), channel_id=1, source_target_pairs={{0,224},{32,0},{64,32},{96,64},{128,96},{160,128},{192,160},{224,1... | collective-permute-start | bytes 442376 | tf_op jit(solution)/shard_map/ppermute | solution.py:22
  35.2 3.1 %collective-permute-done.5 = bf16[2,96,384]{2,1,0:T(8,128)(2,1)S(1)} collective-permute-done((bf16[2,96,384]{2,1,0:T(8,128)(2,1)S(1)}, bf16[2,96,384]{2,1,0:T(8,128)(2,1)S(1)}, u32[]{:S(2)}, u32[]{:S(2)}) %collective-permute-start.5) | collective-permute-done | bytes 147488 | tf_op jit(solution)/shard_map/ppermute | solution.py:22
  38.3 5.4 %collective-permute-done.8.refs_2_ = bf16[768,384]{1,0:T(8,128)(2,1)S(1)} collective-permute-done((bf16[768,384]{1,0:T(8,128)(2,1)}, bf16[768,384]{1,0:T(8,128)(2,1)S(1)}, u32[]{:S(2)}, u32[]{:S(2)}) %collective-permute-start.8) | collective-permute-done | bytes 589856 | tf_op jit(solution)/shard_map/ppermute | solution.py:160
  43.7 3.0 %collective-permute-start.9 = (bf16[2,96,384]{2,1,0:T(8,128)(2,1)S(1)}, bf16[2,96,384]{2,1,0:T(8,128)(2,1)}, u32[]{:S(2)}, u32[]{:S(2)}) collective-permute-start(bf16[2,96,384]{2,1,0:T(8,128)(2,1)S(1)} %bitcast_select_fusion.3), channel_id=1, source_target_pairs={{0,16},{16,0},{1,17},{17,1},{2,18},{18,2},{3,19},{19,3},{4,20},{20... | collective-permute-start | bytes 442376 | tf_op jit(solution)/shard_map/ppermute | solution.py:168
  46.8 3.7 %collective-permute-done.9 = bf16[2,96,384]{2,1,0:T(8,128)(2,1)} collective-permute-done((bf16[2,96,384]{2,1,0:T(8,128)(2,1)S(1)}, bf16[2,96,384]{2,1,0:T(8,128)(2,1)}, u32[]{:S(2)}, u32[]{:S(2)}) %collective-permute-start.9) | collective-permute-done | bytes 147488 | tf_op jit(solution)/shard_map/ppermute | solution.py:168
  51.7 2.9 %collective-permute-start.15 = (bf16[768,384]{1,0:T(8,128)(2,1)S(1)}, bf16[768,384]{1,0:T(8,128)(2,1)S(1)}, u32[]{:S(2)}, u32[]{:S(2)}) collective-permute-start(bf16[768,384]{1,0:T(8,128)(2,1)S(1)} %broadcast_select_fusion), channel_id=1, source_target_pairs={{0,16},{16,0},{1,17},{17,1},{2,18},{18,2},{3,19},{19,3},{4,20},{20... | collective-permute-start | bytes 1769480 | tf_op jit(solution)/shard_map/ppermute | solution.py:170
  54.7 3.2 %collective-permute-start.12 = (bf16[2,96,384]{2,1,0:T(8,128)(2,1)S(1)}, bf16[2,96,384]{2,1,0:T(8,128)(2,1)}, u32[]{:S(2)}, u32[]{:S(2)}) collective-permute-start(bf16[2,96,384]{2,1,0:T(8,128)(2,1)S(1)} %broadcast_select_fusion.2.refs_2_), channel_id=1, source_target_pairs={{0,224},{32,0},{64,32},{96,64},{128,96},{160,128},{192,160},{224,1... | collective-permute-start | bytes 442376 | tf_op jit(solution)/shard_map/ppermute | solution.py:22
  60.0 7.3 %shard_map.82 = (f32[3,768,1]{2,1,0:T(8,128)S(1)}, f32[3,768,256]{2,1,0:T(8,128)S(1)}) custom-call(s32[7]{0:T(128)S(1)} %stack.27.refs_0_, bf16[16,48,384]{2,1,0:T(8,128)(2,1)S(1)} %bitcast.96, bf16[768,384]{1,0:T(8,128)(2,1)S(1)} %copy-done.2, bf16[768,384]{1,0:T(8,128)(2,1)S(1)} %copy-done.1, bf16[768,384]{1,0:T(8,128)(2,1)S(1)} %copy-done.7, ...), custom_call_target="tpu_custom_call" | custom-call | flops 1811939328 | bytes 5898240 | tf_op jit(solution)/shard_map/pallas_call | solution.py:133
  69.4 3.2 %collective-permute-start.14 = (bf16[2,96,384]{2,1,0:T(8,128)(2,1)}, bf16[2,96,384]{2,1,0:T(8,128)(2,1)}, u32[]{:S(2)}, u32[]{:S(2)}) collective-permute-start(bf16[2,96,384]{2,1,0:T(8,128)(2,1)} %collective-permute-done.12.refs_4_), channel_id=1, source_target_pairs={{0,224},{32,0},{64,32},{96,64},{128,96},{160,128},{192,160},{224,1... | collective-permute-start | bytes 442376 | tf_op jit(solution)/shard_map/ppermute | solution.py:22
  72.6 3.5 %collective-permute-done.13.refs_5_ = bf16[2,96,384]{2,1,0:T(8,128)(2,1)} collective-permute-done((bf16[2,96,384]{2,1,0:T(8,128)(2,1)S(1)}, bf16[2,96,384]{2,1,0:T(8,128)(2,1)}, u32[]{:S(2)}, u32[]{:S(2)}) %collective-permute-start.13) | collective-permute-done | bytes 147488 | tf_op jit(solution)/shard_map/ppermute | solution.py:22
  79.5 3.3 %collective-permute-start.17 = (bf16[2,96,384]{2,1,0:T(8,128)(2,1)}, bf16[2,96,384]{2,1,0:T(8,128)(2,1)S(1)}, u32[]{:S(2)}, u32[]{:S(2)}) collective-permute-start(bf16[2,96,384]{2,1,0:T(8,128)(2,1)} %collective-permute-done.14.refs_6_), channel_id=1, source_target_pairs={{0,224},{32,0},{64,32},{96,64},{128,96},{160,128},{192,160},{224,1... | collective-permute-start | bytes 442376 | tf_op jit(solution)/shard_map/ppermute | solution.py:22
  86.7 4.9 %shard_map.83 = (f32[3,768,1]{2,1,0:T(8,128)S(1)}, f32[3,768,256]{2,1,0:T(8,128)S(1)}) custom-call(s32[7]{0:T(128)S(1)} %stack.27.refs_0_, bf16[16,48,384]{2,1,0:T(8,128)(2,1)S(1)} %bitcast.97, bf16[768,384]{1,0:T(8,128)(2,1)S(1)} %copy-done.9, bf16[768,384]{1,0:T(8,128)(2,1)S(1)} %copy-done.11, f32[3,768,1]{2,1,0:T(8,128)S(1)} %get-tuple-element.44.refs_4_, ...), custom_call_target="tpu_custom_call" | custom-call | flops 905969664 | bytes 5898240 | tf_op jit(solution)/shard_map/pallas_call | solution.py:133
  91.7 3.6 %pad_maximum_fusion = bf16[768,6144]{1,0:T(8,128)(2,1)S(1)} fusion(bf16[384,6144]{1,0:T(8,128)(2,1)} %collective-permute-done.19, bf16[384,6144]{1,0:T(8,128)(2,1)S(1)} %copy-done.16), kind=kLoop, calls=%fused_computation | loop fusion | flops 18874368 | bytes 18874368 | tf_op jit(solution)/shard_map/concatenate | solution.py:211
  95.3 2.9 %collective-permute-done.18.refs_9_ = bf16[2,96,384]{2,1,0:T(8,128)(2,1)S(1)} collective-permute-done((bf16[2,96,384]{2,1,0:T(8,128)(2,1)}, bf16[2,96,384]{2,1,0:T(8,128)(2,1)S(1)}, u32[]{:S(2)}, u32[]{:S(2)}) %collective-permute-start.18) | collective-permute-done | bytes 147488 | tf_op jit(solution)/shard_map/ppermute | solution.py:22
  98.2 6.0 %shard_map.84 = bf16[768,384]{1,0:T(8,128)(2,1)S(1)} custom-call(s32[7]{0:T(128)S(1)} %stack.27.refs_0_, bf16[16,48,384]{2,1,0:T(8,128)(2,1)S(1)} %bitcast.98, bf16[2,96,384]{2,1,0:T(8,128)(2,1)S(1)} %broadcast_select_fusion.2.refs_2_, bf16[2,96,384]{2,1,0:T(8,128)(2,1)S(1)} %copy-done.15, bf16[2,96,384]{2,1,0:T(8,128)(2,1)} %collective-permute-done.12.refs_4_, ...), custom_call_target="tpu_custom_call" | custom-call | flops 905969664 | bytes 5898240 | tf_op jit(solution)/shard_map/pallas_call | solution.py:133
  114.1 4.9 %collective-permute-done.25 = bf16[2,48,1728]{2,1,0:T(8,128)(2,1)S(1)} collective-permute-done((bf16[2,48,1728]{2,1,0:T(8,128)(2,1)S(1)}, bf16[2,48,1728]{2,1,0:T(8,128)(2,1)S(1)}, u32[]{:S(2)}, u32[]{:S(2)}) %collective-permute-start.25) | collective-permute-done | bytes 331808 | tf_op jit(solution)/shard_map/ppermute | solution.py:22
  124.0 11.9 %collective-permute-done.21 = bf16[4,48,2688]{2,1,0:T(8,128)(2,1)S(1)} collective-permute-done((bf16[4,48,2688]{2,1,0:T(8,128)(2,1)S(1)}, bf16[4,48,2688]{2,1,0:T(8,128)(2,1)S(1)}, u32[]{:S(2)}, u32[]{:S(2)}) %collective-permute-start.21) | collective-permute-done | bytes 1032224 | tf_op jit(solution)/shard_map/ppermute | solution.py:241
  142.1 3.4 %collective-permute-done.22 = bf16[48,2688]{1,0:T(8,128)(2,1)S(1)} collective-permute-done((bf16[48,2688]{1,0:T(8,128)(2,1)S(1)}, bf16[48,2688]{1,0:T(8,128)(2,1)S(1)}, u32[]{:S(2)}, u32[]{:S(2)}) %collective-permute-start.22) | collective-permute-done | bytes 258080 | tf_op jit(solution)/shard_map/ppermute | solution.py:22
  145.5 5.9 %collective-permute-done.23 = bf16[48,2688]{1,0:T(8,128)(2,1)S(1)} collective-permute-done((bf16[48,2688]{1,0:T(8,128)(2,1)S(1)}, bf16[48,2688]{1,0:T(8,128)(2,1)S(1)}, u32[]{:S(2)}, u32[]{:S(2)}) %collective-permute-start.23) | collective-permute-done | bytes 258080 | tf_op jit(solution)/shard_map/ppermute | solution.py:22
  (114 shorter events, 42.4 us)
Async XLA Ops:
  0.0 91.7 %collective-permute-start.19 = (bf16[384,6144]{1,0:T(8,128)(2,1)}, bf16[384,6144]{1,0:T(8,128)(2,1)}, u32[]{:S(2)}, u32[]{:S(2)}) collective-permute-start(bf16[384,6144]{1,0:T(8,128)(2,1)} %param.12), channel_id=1, source_target_pairs={{0,1},{1,0},{2,3},{3,2},{4,5},{5,4},{6,7},{7,6},{8,9},{9,8},{10,11... | collective-permute-start | bytes 14155784 | tf_op jit(solution)/shard_map/ppermute | solution.py:211
  1.3 9.6 %collective-permute-start = (bf16[2,96,384]{2,1,0:T(8,128)(2,1)S(1)}, bf16[2,96,384]{2,1,0:T(8,128)(2,1)S(1)}, u32[]{:S(2)}, u32[]{:S(2)}) collective-permute-start(bf16[2,96,384]{2,1,0:T(8,128)(2,1)S(1)} %get-tuple-element.59), channel_id=1, source_target_pairs={{0,224},{32,0},{64,32},{96,64},{128,96},{160,128},{192,160},{224,1... | collective-permute-start | bytes 442376 | tf_op jit(solution)/shard_map/ppermute | solution.py:22
  7.2 16.9 %collective-permute-start.3 = (bf16[768,384]{1,0:T(8,128)(2,1)S(1)}, bf16[768,384]{1,0:T(8,128)(2,1)S(1)}, u32[]{:S(2)}, u32[]{:S(2)}) collective-permute-start(bf16[768,384]{1,0:T(8,128)(2,1)S(1)} %copy-done.2), channel_id=1, source_target_pairs={{0,32},{32,64},{64,96},{96,128},{128,160},{160,192},{192,224},{224... | collective-permute-start | bytes 1769480 | tf_op jit(solution)/shard_map/ppermute | solution.py:22
  24.1 7.7 %collective-permute-start.4 = (bf16[2,96,384]{2,1,0:T(8,128)(2,1)S(1)}, bf16[2,96,384]{2,1,0:T(8,128)(2,1)S(1)}, u32[]{:S(2)}, u32[]{:S(2)}) collective-permute-start(bf16[2,96,384]{2,1,0:T(8,128)(2,1)S(1)} %get-tuple-element.31), channel_id=1, source_target_pairs={{0,32},{32,64},{64,96},{96,128},{128,160},{160,192},{192,224},{224... | collective-permute-start | bytes 442376 | tf_op jit(solution)/shard_map/ppermute | solution.py:22
  24.1 7.7 %collective-permute-start.6 = (bf16[2,96,384]{2,1,0:T(8,128)(2,1)S(1)}, bf16[2,96,384]{2,1,0:T(8,128)(2,1)S(1)}, u32[]{:S(2)}, u32[]{:S(2)}) collective-permute-start(bf16[2,96,384]{2,1,0:T(8,128)(2,1)S(1)} %fusion.17), channel_id=1, source_target_pairs={{0,224},{32,0},{64,32},{96,64},{128,96},{160,128},{192,160},{224,1... | collective-permute-start | bytes 442376 | tf_op jit(solution)/shard_map/ppermute | solution.py:22
  28.8 15.0 %collective-permute-start.8 = (bf16[768,384]{1,0:T(8,128)(2,1)}, bf16[768,384]{1,0:T(8,128)(2,1)S(1)}, u32[]{:S(2)}, u32[]{:S(2)}) collective-permute-start(bf16[768,384]{1,0:T(8,128)(2,1)} %broadcast_select_fusion.1), channel_id=1, source_target_pairs={{0,16},{16,0},{1,17},{17,1},{2,18},{18,2},{3,19},{19,3},{4,20},{20... | collective-permute-start | bytes 1769480 | tf_op jit(solution)/shard_map/ppermute | solution.py:160
  38.3 13.3 %collective-permute-start.10 = (bf16[768,384]{1,0:T(8,128)(2,1)S(1)}, bf16[768,384]{1,0:T(8,128)(2,1)S(1)}, u32[]{:S(2)}, u32[]{:S(2)}) collective-permute-start(bf16[768,384]{1,0:T(8,128)(2,1)S(1)} %copy-done.1), channel_id=1, source_target_pairs={{0,32},{32,64},{64,96},{96,128},{128,160},{160,192},{192,224},{224... | collective-permute-start | bytes 1769480 | tf_op jit(solution)/shard_map/ppermute | solution.py:22
  43.7 6.8 %collective-permute-start.9 = (bf16[2,96,384]{2,1,0:T(8,128)(2,1)S(1)}, bf16[2,96,384]{2,1,0:T(8,128)(2,1)}, u32[]{:S(2)}, u32[]{:S(2)}) collective-permute-start(bf16[2,96,384]{2,1,0:T(8,128)(2,1)S(1)} %bitcast_select_fusion.3), channel_id=1, source_target_pairs={{0,16},{16,0},{1,17},{17,1},{2,18},{18,2},{3,19},{19,3},{4,20},{20... | collective-permute-start | bytes 442376 | tf_op jit(solution)/shard_map/ppermute | solution.py:168
  51.7 24.4 %collective-permute-start.15 = (bf16[768,384]{1,0:T(8,128)(2,1)S(1)}, bf16[768,384]{1,0:T(8,128)(2,1)S(1)}, u32[]{:S(2)}, u32[]{:S(2)}) collective-permute-start(bf16[768,384]{1,0:T(8,128)(2,1)S(1)} %broadcast_select_fusion), channel_id=1, source_target_pairs={{0,16},{16,0},{1,17},{17,1},{2,18},{18,2},{3,19},{19,3},{4,20},{20... | collective-permute-start | bytes 1769480 | tf_op jit(solution)/shard_map/ppermute | solution.py:170
  54.7 14.1 %collective-permute-start.11 = (bf16[2,96,384]{2,1,0:T(8,128)(2,1)S(1)}, bf16[2,96,384]{2,1,0:T(8,128)(2,1)S(1)}, u32[]{:S(2)}, u32[]{:S(2)}) collective-permute-start(bf16[2,96,384]{2,1,0:T(8,128)(2,1)S(1)} %broadcast_select_fusion.2.refs_2_), channel_id=1, source_target_pairs={{0,32},{32,64},{64,96},{96,128},{128,160},{160,192},{192,224},{224... | collective-permute-start | bytes 442376 | tf_op jit(solution)/shard_map/ppermute | solution.py:22
  54.7 14.7 %collective-permute-start.12 = (bf16[2,96,384]{2,1,0:T(8,128)(2,1)S(1)}, bf16[2,96,384]{2,1,0:T(8,128)(2,1)}, u32[]{:S(2)}, u32[]{:S(2)}) collective-permute-start(bf16[2,96,384]{2,1,0:T(8,128)(2,1)S(1)} %broadcast_select_fusion.2.refs_2_), channel_id=1, source_target_pairs={{0,224},{32,0},{64,32},{96,64},{128,96},{160,128},{192,160},{224,1... | collective-permute-start | bytes 442376 | tf_op jit(solution)/shard_map/ppermute | solution.py:22
  68.7 7.4 %collective-permute-start.13 = (bf16[2,96,384]{2,1,0:T(8,128)(2,1)S(1)}, bf16[2,96,384]{2,1,0:T(8,128)(2,1)}, u32[]{:S(2)}, u32[]{:S(2)}) collective-permute-start(bf16[2,96,384]{2,1,0:T(8,128)(2,1)S(1)} %collective-permute-done.11.refs_3_), channel_id=1, source_target_pairs={{0,32},{32,64},{64,96},{96,128},{128,160},{160,192},{192,224},{224... | collective-permute-start | bytes 442376 | tf_op jit(solution)/shard_map/ppermute | solution.py:22
  69.4 10.1 %collective-permute-start.14 = (bf16[2,96,384]{2,1,0:T(8,128)(2,1)}, bf16[2,96,384]{2,1,0:T(8,128)(2,1)}, u32[]{:S(2)}, u32[]{:S(2)}) collective-permute-start(bf16[2,96,384]{2,1,0:T(8,128)(2,1)} %collective-permute-done.12.refs_4_), channel_id=1, source_target_pairs={{0,224},{32,0},{64,32},{96,64},{128,96},{160,128},{192,160},{224,1... | collective-permute-start | bytes 442376 | tf_op jit(solution)/shard_map/ppermute | solution.py:22
  77.0 14.6 %collective-permute-start.16 = (bf16[2,96,384]{2,1,0:T(8,128)(2,1)}, bf16[2,96,384]{2,1,0:T(8,128)(2,1)}, u32[]{:S(2)}, u32[]{:S(2)}) collective-permute-start(bf16[2,96,384]{2,1,0:T(8,128)(2,1)} %collective-permute-done.13.refs_5_), channel_id=1, source_target_pairs={{0,32},{32,64},{64,96},{96,128},{128,160},{160,192},{192,224},{224... | collective-permute-start | bytes 442376 | tf_op jit(solution)/shard_map/ppermute | solution.py:22
  79.5 15.7 %collective-permute-start.17 = (bf16[2,96,384]{2,1,0:T(8,128)(2,1)}, bf16[2,96,384]{2,1,0:T(8,128)(2,1)S(1)}, u32[]{:S(2)}, u32[]{:S(2)}) collective-permute-start(bf16[2,96,384]{2,1,0:T(8,128)(2,1)} %collective-permute-done.14.refs_6_), channel_id=1, source_target_pairs={{0,224},{32,0},{64,32},{96,64},{128,96},{160,128},{192,160},{224,1... | collective-permute-start | bytes 442376 | tf_op jit(solution)/shard_map/ppermute | solution.py:22
  108.8 10.2 %collective-permute-start.25 = (bf16[2,48,1728]{2,1,0:T(8,128)(2,1)S(1)}, bf16[2,48,1728]{2,1,0:T(8,128)(2,1)S(1)}, u32[]{:S(2)}, u32[]{:S(2)}) collective-permute-start(bf16[2,48,1728]{2,1,0:T(8,128)(2,1)S(1)} %get-tuple-element.63), channel_id=1, source_target_pairs={{0,4},{4,8},{8,12},{12,0},{1,5},{5,9},{9,13},{13,1},{2,6},{6,10},{... | collective-permute-start | bytes 995336 | tf_op jit(solution)/shard_map/ppermute | solution.py:22
  111.2 24.7 %collective-permute-start.21 = (bf16[4,48,2688]{2,1,0:T(8,128)(2,1)S(1)}, bf16[4,48,2688]{2,1,0:T(8,128)(2,1)S(1)}, u32[]{:S(2)}, u32[]{:S(2)}) collective-permute-start(bf16[4,48,2688]{2,1,0:T(8,128)(2,1)S(1)} %bitcast.103), channel_id=1, source_target_pairs={{0,2},{2,0},{1,3},{3,1},{4,6},{6,4},{5,7},{7,5},{8,10},{10,8},{9,1... | collective-permute-start | bytes 3096584 | tf_op jit(solution)/shard_map/ppermute | solution.py:241
  112.2 10.9 %collective-permute-start.27 = (bf16[2,48,1728]{2,1,0:T(8,128)(2,1)S(1)}, bf16[2,48,1728]{2,1,0:T(8,128)(2,1)S(1)}, u32[]{:S(2)}, u32[]{:S(2)}) collective-permute-start(bf16[2,48,1728]{2,1,0:T(8,128)(2,1)S(1)} %get-tuple-element.64), channel_id=1, source_target_pairs={{0,12},{4,0},{8,4},{12,8},{1,13},{5,1},{9,5},{13,9},{2,14},{6,2},{... | collective-permute-start | bytes 995336 | tf_op jit(solution)/shard_map/ppermute | solution.py:22
  119.3 21.6 %collective-permute-start.26 = (bf16[2,48,3456]{2,1,0:T(8,128)(2,1)S(1)}, bf16[2,48,3456]{2,1,0:T(8,128)(2,1)S(1)}, u32[]{:S(2)}, u32[]{:S(2)}) collective-permute-start(bf16[2,48,3456]{2,1,0:T(8,128)(2,1)S(1)} %pad_maximum_fusion.1), channel_id=1, source_target_pairs={{0,4},{4,8},{8,12},{12,0},{1,5},{5,9},{9,13},{13,1},{2,6},{6,10},{... | collective-permute-start | bytes 1990664 | tf_op jit(solution)/shard_map/ppermute | solution.py:22
  123.5 17.4 %collective-permute-start.28 = (bf16[2,48,3456]{2,1,0:T(8,128)(2,1)S(1)}, bf16[2,48,3456]{2,1,0:T(8,128)(2,1)S(1)}, u32[]{:S(2)}, u32[]{:S(2)}) collective-permute-start(bf16[2,48,3456]{2,1,0:T(8,128)(2,1)S(1)} %pad_maximum_fusion.2), channel_id=1, source_target_pairs={{0,12},{4,0},{8,4},{12,8},{1,13},{5,1},{9,5},{13,9},{2,14},{6,2},{... | collective-permute-start | bytes 1990664 | tf_op jit(solution)/shard_map/ppermute | solution.py:22
  136.2 9.2 %collective-permute-start.22 = (bf16[48,2688]{1,0:T(8,128)(2,1)S(1)}, bf16[48,2688]{1,0:T(8,128)(2,1)S(1)}, u32[]{:S(2)}, u32[]{:S(2)}) collective-permute-start(bf16[48,2688]{1,0:T(8,128)(2,1)S(1)} %get-tuple-element.60), channel_id=1, source_target_pairs={{0,4},{4,8},{8,12},{12,0},{1,5},{5,9},{9,13},{13,1},{2,6},{6,10},{... | collective-permute-start | bytes 774152 | tf_op jit(solution)/shard_map/ppermute | solution.py:22
  137.8 13.6 %collective-permute-start.23 = (bf16[48,2688]{1,0:T(8,128)(2,1)S(1)}, bf16[48,2688]{1,0:T(8,128)(2,1)S(1)}, u32[]{:S(2)}, u32[]{:S(2)}) collective-permute-start(bf16[48,2688]{1,0:T(8,128)(2,1)S(1)} %get-tuple-element.62), channel_id=1, source_target_pairs={{0,12},{4,0},{8,4},{12,8},{1,13},{5,1},{9,5},{13,9},{2,14},{6,2},{... | collective-permute-start | bytes 774152 | tf_op jit(solution)/shard_map/ppermute | solution.py:22
  138.3 13.1 %collective-permute-start.24 = (bf16[48,2688]{1,0:T(8,128)(2,1)S(1)}, bf16[48,2688]{1,0:T(8,128)(2,1)S(1)}, u32[]{:S(2)}, u32[]{:S(2)}) collective-permute-start(bf16[48,2688]{1,0:T(8,128)(2,1)S(1)} %get-tuple-element.61), channel_id=1, source_target_pairs={{0,8},{4,12},{8,0},{12,4},{1,9},{5,13},{9,1},{13,5},{2,10},{6,14},... | collective-permute-start | bytes 774152 | tf_op jit(solution)/shard_map/ppermute | solution.py:22
  141.0 10.6 %collective-permute-start.29 = (bf16[48,3456]{1,0:T(8,128)(2,1)S(1)}, bf16[48,3456]{1,0:T(8,128)(2,1)S(1)}, u32[]{:S(2)}, u32[]{:S(2)}) collective-permute-start(bf16[48,3456]{1,0:T(8,128)(2,1)S(1)} %fusion.5), channel_id=1, source_target_pairs={{0,2},{2,0},{1,3},{3,1},{4,6},{6,4},{5,7},{7,5},{8,10},{10,8},{9,1... | collective-permute-start | bytes 995336 | tf_op jit(solution)/shard_map/ppermute | solution.py:245
  (27 other events, 254.3 us)

commit v2 on v0

--- a/solution.py
+++ b/solution.py
@@ -47,6 +47,8 @@
 
         blocks = [clean]
     else:
+        if len(refs) == 1:
+            refs = [refs[0].at[0], refs[0].at[1]]
         blocks = list(zip(refs[::2], refs[1::2]))
     factor = HD ** (-0.5) * LOG2E
     tile = probs_ref.shape[1]
@@ -157,31 +159,28 @@
         if number == UP + 4:
             down, lag2_keys = lax.optimization_barrier((down, lag2_keys))
         down = shift(jnp.where(at_root, own[number], down), "z", NZ, -1)
-    lag1_keys = lax.ppermute(jnp.where(xh == 0, keys, lag2_keys), "xh", SWAP)
     up, lag2_keys = lax.optimization_barrier((own[UP], lag2_keys))
     for number in range(UP, 0, -1):
         up = shift(jnp.where(at_root, own[number], up) if number < UP else up, "z", NZ, 1)
     values_late, up = lax.optimization_barrier((values, up))
     lag2_values = shift(values_late, "z", NZ, 1)
     piece = jnp.where(at_root, own[0], jnp.where(distance <= UP, up, down))
-    piece, lag1_keys = lax.optimization_barrier((piece, lag1_keys))
     piece = jnp.where(xh == lax.rem(root, NXH), piece, lax.ppermute(piece, "xh", SWAP))
     piece, lag2_values = lax.optimization_barrier((piece, lag2_values))
-    lag1_values = lax.ppermute(jnp.where(xh == 0, values, lag2_values), "xh", SWAP)
+    lag1 = jnp.where(xh == 0, jnp.stack([keys, values]), jnp.stack([lag2_keys, lag2_values]))
+    lag1 = lax.ppermute(lag1, "xh", SWAP)
     peak, total = first_pass(scalars, [lag2_keys, lag2_values])
     pieces = [piece]
     up = down = piece
     for number in range(4):
         if number == 1:
             up, peak = lax.optimization_barrier((up, peak))
-        if number == 2:
-            up, lag1_values = lax.optimization_barrier((up, lag1_values))
         up = shift(up, "z", NZ, 1)
         pieces.append(up)
         if number < 3:
             down = shift(down, "z", NZ, -1)
             pieces.append(down)
-    return [peak, total], [lag1_keys, lag1_values], pieces, scalars
+    return [peak, total], lag1, pieces, scalars
 
 
 def add(*terms):
@@ -225,8 +224,8 @@
         return attend(scalars, queries, (0, 1), [keys, values, *lag2])
 
     state, lag1, pieces, scalars = fetch(keys, values, clean_root, z, xh, scalars, first_pass)
-    state = attend(scalars, queries, (2,), lag1, state)
     state, weight = lax.optimization_barrier((state, weight))
+    state = attend(scalars, queries, (2,), [lag1], state)
     attended = attend(scalars, queries, (3,), pieces, state, last=True)
     taken = lax.ppermute(attended[rows // 2 :], "c", SWAP)
     both = jnp.concatenate([attended[: rows // 2], taken], axis=1)

time: 151 us -> 149 us (0.987)
  the two profiles are of different devices: /device:TPU:28 before, /device:TPU:92 now
where the time goes in v2:
time: 149 us; the launch traced here: 147 us
  waiting for transfers between devices  72.3 us (49%)
  starting transfers between devices  28.6 us (19%)
  Pallas kernels  18.1 us (12%)
  other arithmetic  10.5 us (7%)
  local copies, waits for them, and re-layouts  7.38 us (5%)
  between operations  5.7 us (4%)
  matrix products  4.27 us (3%)
    ppermute x23, waiting for transfers between devices, shift(): lax.ppermute(value, axis, [(i, (i + steps) % count) for i in range(count)])  45.4 us
    ppermute x23, starting transfers between devices, shift(): lax.ppermute(value, axis, [(i, (i + steps) % count) for i in range(count)])  24.7 us
    pallas_call x3, Pallas kernels, attend(): pl.pallas_call(functools.partial(attend_body, fresh, last, flags), out_sh...  18.1 us
    ppermute x1, waiting for transfers between devices, local(): x_got = lax.ppermute(x_first[1], 'xl', SWAP)  11.4 us
    ppermute x1, waiting for transfers between devices, fetch(): lag1 = lax.ppermute(lag1, 'xh', SWAP)  7.78 us
    ppermute x1, waiting for transfers between devices, fetch(): lax.ppermute(piece, 'xh', SWAP)  6.14 us
    concatenate x1, other arithmetic, local(): jnp.concatenate([out_weight, lax.ppermute(out_weight, 'c', SWAP)], axis=0)  4.99 us
    dot_general x2, matrix products, project(): jnp.dot(both, weight[:, low:high], preferred_element_type=jnp.float32)  4.27 us
  transfers between devices with their start and end apart: 29, of which 18 were waited for; matrix products, arithmetic and copies ran while one was open for 10% of the time, Pallas kernels for 8%

profile of v2, /device:TPU:92, one launch (start us, length us, event | category | flops | bytes accessed | tf_op | source)
XLA Modules:
  0.0 146.9 jit_solution(13577805024006786285)
XLA Ops:
  1.5 1.9 %collective-permute-start.3 = (bf16[768,384]{1,0:T(8,128)(2,1)S(1)}, bf16[768,384]{1,0:T(8,128)(2,1)S(1)}, u32[]{:S(2)}, u32[]{:S(2)}) collective-permute-start(bf16[768,384]{1,0:T(8,128)(2,1)S(1)} %copy-done.2), channel_id=1, source_target_pairs={{0,32},{32,64},{64,96},{96,128},{128,160},{160,192},{192,224},{224... | collective-permute-start | bytes 1769480 | tf_op jit(solution)/shard_map/ppermute | solution.py:22
  10.6 4.1 %collective-permute-done.1 = bf16[2,96,384]{2,1,0:T(8,128)(2,1)S(1)} collective-permute-done((bf16[2,96,384]{2,1,0:T(8,128)(2,1)S(1)}, bf16[2,96,384]{2,1,0:T(8,128)(2,1)S(1)}, u32[]{:S(2)}, u32[]{:S(2)}) %collective-permute-start.1) | collective-permute-done | bytes 147488 | tf_op jit(solution)/shard_map/ppermute | solution.py:22
  14.9 6.1 %collective-permute-done.2 = bf16[2,96,384]{2,1,0:T(8,128)(2,1)S(1)} collective-permute-done((bf16[2,96,384]{2,1,0:T(8,128)(2,1)S(1)}, bf16[2,96,384]{2,1,0:T(8,128)(2,1)S(1)}, u32[]{:S(2)}, u32[]{:S(2)}) %collective-permute-start.2) | collective-permute-done | bytes 147488 | tf_op jit(solution)/shard_map/ppermute | solution.py:22
  20.9 3.2 %collective-permute-start.4 = (bf16[2,96,384]{2,1,0:T(8,128)(2,1)S(1)}, bf16[2,96,384]{2,1,0:T(8,128)(2,1)S(1)}, u32[]{:S(2)}, u32[]{:S(2)}) collective-permute-start(bf16[2,96,384]{2,1,0:T(8,128)(2,1)S(1)} %get-tuple-element.27), channel_id=1, source_target_pairs={{0,32},{32,64},{64,96},{96,128},{128,160},{160,192},{192,224},{224... | collective-permute-start | bytes 442376 | tf_op jit(solution)/shard_map/ppermute | solution.py:22
  24.3 2.6 %collective-permute-done.4 = bf16[2,96,384]{2,1,0:T(8,128)(2,1)S(1)} collective-permute-done((bf16[2,96,384]{2,1,0:T(8,128)(2,1)S(1)}, bf16[2,96,384]{2,1,0:T(8,128)(2,1)S(1)}, u32[]{:S(2)}, u32[]{:S(2)}) %collective-permute-start.4) | collective-permute-done | bytes 147488 | tf_op jit(solution)/shard_map/ppermute | solution.py:22
  26.8 2.6 %collective-permute-done.6 = bf16[2,96,384]{2,1,0:T(8,128)(2,1)S(1)} collective-permute-done((bf16[2,96,384]{2,1,0:T(8,128)(2,1)S(1)}, bf16[2,96,384]{2,1,0:T(8,128)(2,1)S(1)}, u32[]{:S(2)}, u32[]{:S(2)}) %collective-permute-start.6) | collective-permute-done | bytes 147488 | tf_op jit(solution)/shard_map/ppermute | solution.py:22
  31.6 4.7 %collective-permute-done.5 = bf16[2,96,384]{2,1,0:T(8,128)(2,1)S(1)} collective-permute-done((bf16[2,96,384]{2,1,0:T(8,128)(2,1)S(1)}, bf16[2,96,384]{2,1,0:T(8,128)(2,1)S(1)}, u32[]{:S(2)}, u32[]{:S(2)}) %collective-permute-start.5) | collective-permute-done | bytes 147488 | tf_op jit(solution)/shard_map/ppermute | solution.py:22
  37.8 6.1 %collective-permute-done.8 = bf16[2,96,384]{2,1,0:T(8,128)(2,1)S(1)} collective-permute-done((bf16[2,96,384]{2,1,0:T(8,128)(2,1)S(1)}, bf16[2,96,384]{2,1,0:T(8,128)(2,1)S(1)}, u32[]{:S(2)}, u32[]{:S(2)}) %collective-permute-start.8) | collective-permute-done | bytes 147488 | tf_op jit(solution)/shard_map/ppermute | solution.py:168
  44.0 4.6 %collective-permute-done.9.refs_5_ = bf16[768,384]{1,0:T(8,128)(2,1)S(1)} collective-permute-done((bf16[768,384]{1,0:T(8,128)(2,1)S(1)}, bf16[768,384]{1,0:T(8,128)(2,1)S(1)}, u32[]{:S(2)}, u32[]{:S(2)}) %collective-permute-start.9) | collective-permute-done | bytes 589856 | tf_op jit(solution)/shard_map/ppermute | solution.py:22
  53.6 7.3 %shard_map.82 = (f32[3,768,1]{2,1,0:T(8,128)S(1)}, f32[3,768,256]{2,1,0:T(8,128)S(1)}) custom-call(s32[7]{0:T(128)S(1)} %stack.45.refs_0_, bf16[16,48,384]{2,1,0:T(8,128)(2,1)S(1)} %bitcast.102, bf16[768,384]{1,0:T(8,128)(2,1)S(1)} %copy-done.2, bf16[768,384]{1,0:T(8,128)(2,1)S(1)} %copy-done.1, bf16[768,384]{1,0:T(8,128)(2,1)S(1)} %copy-done.7, ...), custom_call_target="tpu_custom_call" | custom-call | flops 1811939328 | bytes 5898240 | tf_op jit(solution)/shard_map/pallas_call | solution.py:135
  64.8 2.4 %collective-permute-done.12.refs_5_ = bf16[2,96,384]{2,1,0:T(8,128)(2,1)} collective-permute-done((bf16[2,96,384]{2,1,0:T(8,128)(2,1)S(1)}, bf16[2,96,384]{2,1,0:T(8,128)(2,1)}, u32[]{:S(2)}, u32[]{:S(2)}) %collective-permute-start.12) | collective-permute-done | bytes 147488 | tf_op jit(solution)/shard_map/ppermute | solution.py:22
  73.4 5.0 %pad_maximum_fusion = bf16[768,6144]{1,0:T(8,128)(2,1)S(1)} fusion(bf16[384,6144]{1,0:T(8,128)(2,1)} %collective-permute-done.18, bf16[384,6144]{1,0:T(8,128)(2,1)} %param.12), kind=kLoop, calls=%fused_computation | loop fusion | flops 18874368 | bytes 18874368 | tf_op jit(solution)/shard_map/concatenate | solution.py:210
  78.5 7.8 %collective-permute-done.17.refs_2_ = bf16[2,768,384]{2,1,0:T(8,128)(2,1)S(1)} collective-permute-done((bf16[2,768,384]{2,1,0:T(8,128)(2,1)}, bf16[2,768,384]{2,1,0:T(8,128)(2,1)S(1)}, u32[]{:S(2)}, u32[]{:S(2)}) %collective-permute-start.17) | collective-permute-done | bytes 1179680 | tf_op jit(solution)/shard_map/ppermute | solution.py:171
  86.2 4.8 %shard_map.83 = (f32[3,768,1]{2,1,0:T(8,128)S(1)}, f32[3,768,256]{2,1,0:T(8,128)S(1)}) custom-call(s32[7]{0:T(128)S(1)} %stack.45.refs_0_, bf16[16,48,384]{2,1,0:T(8,128)(2,1)S(1)} %bitcast.103, bf16[2,768,384]{2,1,0:T(8,128)(2,1)S(1)} %collective-permute-done.17.refs_2_, f32[3,768,1]{2,1,0:T(8,128)S(1)} %get-tuple-element.38.refs_3_, ...), custom_call_target="tpu_custom_call" | custom-call | flops 905969664 | bytes 5898240 | tf_op jit(solution)/shard_map/pallas_call | solution.py:135
  91.1 6.0 %shard_map.84 = bf16[768,384]{1,0:T(8,128)(2,1)S(1)} custom-call(s32[7]{0:T(128)S(1)} %stack.45.refs_0_, bf16[16,48,384]{2,1,0:T(8,128)(2,1)S(1)} %bitcast.104, bf16[2,96,384]{2,1,0:T(8,128)(2,1)S(1)} %broadcast_select_fusion.refs_2_, bf16[2,96,384]{2,1,0:T(8,128)(2,1)S(1)} %copy-done.11, bf16[2,96,384]{2,1,0:T(8,128)(2,1)} %collective-permute-done.11.refs_4_, ...), custom_call_target="tpu_custom_call" | custom-call | flops 905969664 | bytes 5898240 | tf_op jit(solution)/shard_map/pallas_call | solution.py:135
  99.1 2.4 %convolution_convert_fusion = bf16[384,3456]{1,0:T(8,128)(2,1)S(1)} fusion(bf16[768,6144]{1,0:T(8,128)(2,1)S(1)} %pad_maximum_fusion, bf16[384,384]{1,0:T(8,128)(2,1)S(1)} %collective-permute-done.19, bf16[384,384]{1,0:T(8,128)(2,1)S(1)} %get-tuple-element.57), kind=kOutput, calls=%fused_computation.1 | convolution fusion | flops 2040938496 | bytes 8552448 | tf_op jit(solution)/shard_map/dot_general | solution.py:234
  102.0 1.9 %convolution_convert_fusion.1 = bf16[384,2688]{1,0:T(8,128)(2,1)S(1)} fusion(bf16[768,6144]{1,0:T(8,128)(2,1)S(1)} %pad_maximum_fusion, bf16[384,384]{1,0:T(8,128)(2,1)S(1)} %collective-permute-done.19, bf16[384,384]{1,0:T(8,128)(2,1)S(1)} %get-tuple-element.57), kind=kOutput, calls=%fused_computation.3 | convolution fusion | flops 1587658752 | bytes 6782976 | tf_op jit(solution)/shard_map/dot_general | solution.py:234
  105.6 1.9 %collective-permute-start.26 = (bf16[2,48,1728]{2,1,0:T(8,128)(2,1)S(1)}, bf16[2,48,1728]{2,1,0:T(8,128)(2,1)S(1)}, u32[]{:S(2)}, u32[]{:S(2)}) collective-permute-start(bf16[2,48,1728]{2,1,0:T(8,128)(2,1)S(1)} %get-tuple-element.56), channel_id=1, source_target_pairs={{0,12},{4,0},{8,4},{12,8},{1,13},{5,1},{9,5},{13,9},{2,14},{6,2},{... | collective-permute-start | bytes 995336 | tf_op jit(solution)/shard_map/ppermute | solution.py:22
  107.5 4.5 %collective-permute-done.24 = bf16[2,48,1728]{2,1,0:T(8,128)(2,1)S(1)} collective-permute-done((bf16[2,48,1728]{2,1,0:T(8,128)(2,1)S(1)}, bf16[2,48,1728]{2,1,0:T(8,128)(2,1)S(1)}, u32[]{:S(2)}, u32[]{:S(2)}) %collective-permute-start.24) | collective-permute-done | bytes 331808 | tf_op jit(solution)/shard_map/ppermute | solution.py:22
  113.8 2.7 %collective-permute-done.26 = bf16[2,48,1728]{2,1,0:T(8,128)(2,1)S(1)} collective-permute-done((bf16[2,48,1728]{2,1,0:T(8,128)(2,1)S(1)}, bf16[2,48,1728]{2,1,0:T(8,128)(2,1)S(1)}, u32[]{:S(2)}, u32[]{:S(2)}) %collective-permute-start.26) | collective-permute-done | bytes 331808 | tf_op jit(solution)/shard_map/ppermute | solution.py:22
  117.4 11.4 %collective-permute-done.20 = bf16[4,48,2688]{2,1,0:T(8,128)(2,1)S(1)} collective-permute-done((bf16[4,48,2688]{2,1,0:T(8,128)(2,1)S(1)}, bf16[4,48,2688]{2,1,0:T(8,128)(2,1)S(1)}, u32[]{:S(2)}, u32[]{:S(2)}) %collective-permute-start.20) | collective-permute-done | bytes 1032224 | tf_op jit(solution)/shard_map/ppermute | solution.py:240
  131.2 2.5 %collective-permute-start.23 = (bf16[48,2688]{1,0:T(8,128)(2,1)S(1)}, bf16[48,2688]{1,0:T(8,128)(2,1)S(1)}, u32[]{:S(2)}, u32[]{:S(2)}) collective-permute-start(bf16[48,2688]{1,0:T(8,128)(2,1)S(1)} %get-tuple-element.53), channel_id=1, source_target_pairs={{0,8},{4,12},{8,0},{12,4},{1,9},{5,13},{9,1},{13,5},{2,10},{6,14},... | collective-permute-start | bytes 774152 | tf_op jit(solution)/shard_map/ppermute | solution.py:22
  135.2 3.2 %collective-permute-done.21 = bf16[48,2688]{1,0:T(8,128)(2,1)S(1)} collective-permute-done((bf16[48,2688]{1,0:T(8,128)(2,1)S(1)}, bf16[48,2688]{1,0:T(8,128)(2,1)S(1)}, u32[]{:S(2)}, u32[]{:S(2)}) %collective-permute-start.21) | collective-permute-done | bytes 258080 | tf_op jit(solution)/shard_map/ppermute | solution.py:22
  138.4 6.3 %collective-permute-done.22 = bf16[48,2688]{1,0:T(8,128)(2,1)S(1)} collective-permute-done((bf16[48,2688]{1,0:T(8,128)(2,1)S(1)}, bf16[48,2688]{1,0:T(8,128)(2,1)S(1)}, u32[]{:S(2)}, u32[]{:S(2)}) %collective-permute-start.22) | collective-permute-done | bytes 258080 | tf_op jit(solution)/shard_map/ppermute | solution.py:22
  (99 shorter events, 35.3 us)
Async XLA Ops:
  0.0 73.4 %collective-permute-start.18 = (bf16[384,6144]{1,0:T(8,128)(2,1)}, bf16[384,6144]{1,0:T(8,128)(2,1)}, u32[]{:S(2)}, u32[]{:S(2)}) collective-permute-start(bf16[384,6144]{1,0:T(8,128)(2,1)} %param.12), channel_id=1, source_target_pairs={{0,1},{1,0},{2,3},{3,2},{4,5},{5,4},{6,7},{7,6},{8,9},{9,8},{10,11... | collective-permute-start | bytes 14155784 | tf_op jit(solution)/shard_map/ppermute | solution.py:210
  1.3 6.4 %collective-permute-start = (bf16[2,96,384]{2,1,0:T(8,128)(2,1)S(1)}, bf16[2,96,384]{2,1,0:T(8,128)(2,1)S(1)}, u32[]{:S(2)}, u32[]{:S(2)}) collective-permute-start(bf16[2,96,384]{2,1,0:T(8,128)(2,1)S(1)} %get-tuple-element.50), channel_id=1, source_target_pairs={{0,224},{32,0},{64,32},{96,64},{128,96},{160,128},{192,160},{224,1... | collective-permute-start | bytes 442376 | tf_op jit(solution)/shard_map/ppermute | solution.py:22
  1.5 19.5 %collective-permute-start.3 = (bf16[768,384]{1,0:T(8,128)(2,1)S(1)}, bf16[768,384]{1,0:T(8,128)(2,1)S(1)}, u32[]{:S(2)}, u32[]{:S(2)}) collective-permute-start(bf16[768,384]{1,0:T(8,128)(2,1)S(1)} %copy-done.2), channel_id=1, source_target_pairs={{0,32},{32,64},{64,96},{96,128},{128,160},{160,192},{192,224},{224... | collective-permute-start | bytes 1769480 | tf_op jit(solution)/shard_map/ppermute | solution.py:22
  7.7 7.0 %collective-permute-start.1 = (bf16[2,96,384]{2,1,0:T(8,128)(2,1)S(1)}, bf16[2,96,384]{2,1,0:T(8,128)(2,1)S(1)}, u32[]{:S(2)}, u32[]{:S(2)}) collective-permute-start(bf16[2,96,384]{2,1,0:T(8,128)(2,1)S(1)} %bitcast_select_fusion.4), channel_id=1, source_target_pairs={{0,224},{32,0},{64,32},{96,64},{128,96},{160,128},{192,160},{224,1... | collective-permute-start | bytes 442376 | tf_op jit(solution)/shard_map/ppermute | solution.py:22
  29.5 6.8 %collective-permute-start.5 = (bf16[2,96,384]{2,1,0:T(8,128)(2,1)S(1)}, bf16[2,96,384]{2,1,0:T(8,128)(2,1)S(1)}, u32[]{:S(2)}, u32[]{:S(2)}) collective-permute-start(bf16[2,96,384]{2,1,0:T(8,128)(2,1)S(1)} %get-tuple-element.49), channel_id=1, source_target_pairs={{0,32},{32,64},{64,96},{96,128},{128,160},{160,192},{192,224},{224... | collective-permute-start | bytes 442376 | tf_op jit(solution)/shard_map/ppermute | solution.py:22
  30.8 6.4 %collective-permute-start.7 = (bf16[2,96,384]{2,1,0:T(8,128)(2,1)S(1)}, bf16[2,96,384]{2,1,0:T(8,128)(2,1)S(1)}, u32[]{:S(2)}, u32[]{:S(2)}) collective-permute-start(bf16[2,96,384]{2,1,0:T(8,128)(2,1)S(1)} %get-tuple-element.48), channel_id=1, source_target_pairs={{0,224},{32,0},{64,32},{96,64},{128,96},{160,128},{192,160},{224,1... | collective-permute-start | bytes 442376 | tf_op jit(solution)/shard_map/ppermute | solution.py:22
  36.3 12.3 %collective-permute-start.9 = (bf16[768,384]{1,0:T(8,128)(2,1)S(1)}, bf16[768,384]{1,0:T(8,128)(2,1)S(1)}, u32[]{:S(2)}, u32[]{:S(2)}) collective-permute-start(bf16[768,384]{1,0:T(8,128)(2,1)S(1)} %copy-done.1), channel_id=1, source_target_pairs={{0,32},{32,64},{64,96},{96,128},{128,160},{160,192},{192,224},{224... | collective-permute-start | bytes 1769480 | tf_op jit(solution)/shard_map/ppermute | solution.py:22
  37.2 6.7 %collective-permute-start.8 = (bf16[2,96,384]{2,1,0:T(8,128)(2,1)S(1)}, bf16[2,96,384]{2,1,0:T(8,128)(2,1)S(1)}, u32[]{:S(2)}, u32[]{:S(2)}) collective-permute-start(bf16[2,96,384]{2,1,0:T(8,128)(2,1)S(1)} %bitcast_select_fusion.3), channel_id=1, source_target_pairs={{0,16},{16,0},{1,17},{17,1},{2,18},{18,2},{3,19},{19,3},{4,20},{20... | collective-permute-start | bytes 442376 | tf_op jit(solution)/shard_map/ppermute | solution.py:168
  49.4 11.4 %collective-permute-start.10 = (bf16[2,96,384]{2,1,0:T(8,128)(2,1)S(1)}, bf16[2,96,384]{2,1,0:T(8,128)(2,1)S(1)}, u32[]{:S(2)}, u32[]{:S(2)}) collective-permute-start(bf16[2,96,384]{2,1,0:T(8,128)(2,1)S(1)} %broadcast_select_fusion.refs_2_), channel_id=1, source_target_pairs={{0,32},{32,64},{64,96},{96,128},{128,160},{160,192},{192,224},{224... | collective-permute-start | bytes 442376 | tf_op jit(solution)/shard_map/ppermute | solution.py:22
  50.7 13.4 %collective-permute-start.11 = (bf16[2,96,384]{2,1,0:T(8,128)(2,1)S(1)}, bf16[2,96,384]{2,1,0:T(8,128)(2,1)}, u32[]{:S(2)}, u32[]{:S(2)}) collective-permute-start(bf16[2,96,384]{2,1,0:T(8,128)(2,1)S(1)} %broadcast_select_fusion.refs_2_), channel_id=1, source_target_pairs={{0,224},{32,0},{64,32},{96,64},{128,96},{160,128},{192,160},{224,1... | collective-permute-start | bytes 442376 | tf_op jit(solution)/shard_map/ppermute | solution.py:22
  60.9 6.3 %collective-permute-start.12 = (bf16[2,96,384]{2,1,0:T(8,128)(2,1)S(1)}, bf16[2,96,384]{2,1,0:T(8,128)(2,1)}, u32[]{:S(2)}, u32[]{:S(2)}) collective-permute-start(bf16[2,96,384]{2,1,0:T(8,128)(2,1)S(1)} %collective-permute-done.10.refs_3_), channel_id=1, source_target_pairs={{0,32},{32,64},{64,96},{96,128},{128,160},{160,192},{192,224},{224... | collective-permute-start | bytes 442376 | tf_op jit(solution)/shard_map/ppermute | solution.py:22
  63.5 22.7 %collective-permute-start.17 = (bf16[2,768,384]{2,1,0:T(8,128)(2,1)}, bf16[2,768,384]{2,1,0:T(8,128)(2,1)S(1)}, u32[]{:S(2)}, u32[]{:S(2)}) collective-permute-start(bf16[2,768,384]{2,1,0:T(8,128)(2,1)} %maximum_select_fusion), channel_id=1, source_target_pairs={{0,16},{16,0},{1,17},{17,1},{2,18},{18,2},{3,19},{19,3},{4,20},{20... | collective-permute-start | bytes 3538952 | tf_op jit(solution)/shard_map/ppermute | solution.py:171
  64.1 6.7 %collective-permute-start.13 = (bf16[2,96,384]{2,1,0:T(8,128)(2,1)}, bf16[2,96,384]{2,1,0:T(8,128)(2,1)}, u32[]{:S(2)}, u32[]{:S(2)}) collective-permute-start(bf16[2,96,384]{2,1,0:T(8,128)(2,1)} %collective-permute-done.11.refs_4_), channel_id=1, source_target_pairs={{0,224},{32,0},{64,32},{96,64},{128,96},{160,128},{192,160},{224,1... | collective-permute-start | bytes 442376 | tf_op jit(solution)/shard_map/ppermute | solution.py:22
  70.7 20.4 %collective-permute-start.15 = (bf16[2,96,384]{2,1,0:T(8,128)(2,1)}, bf16[2,96,384]{2,1,0:T(8,128)(2,1)S(1)}, u32[]{:S(2)}, u32[]{:S(2)}) collective-permute-start(bf16[2,96,384]{2,1,0:T(8,128)(2,1)} %collective-permute-done.13.refs_6_), channel_id=1, source_target_pairs={{0,224},{32,0},{64,32},{96,64},{128,96},{160,128},{192,160},{224,1... | collective-permute-start | bytes 442376 | tf_op jit(solution)/shard_map/ppermute | solution.py:22
  72.6 18.5 %collective-permute-start.16 = (bf16[2,96,384]{2,1,0:T(8,128)(2,1)}, bf16[2,96,384]{2,1,0:T(8,128)(2,1)S(1)}, u32[]{:S(2)}, u32[]{:S(2)}) collective-permute-start(bf16[2,96,384]{2,1,0:T(8,128)(2,1)} %collective-permute-done.14.refs_7_), channel_id=1, source_target_pairs={{0,32},{32,64},{64,96},{96,128},{128,160},{160,192},{192,224},{224... | collective-permute-start | bytes 442376 | tf_op jit(solution)/shard_map/ppermute | solution.py:22
  101.7 10.2 %collective-permute-start.24 = (bf16[2,48,1728]{2,1,0:T(8,128)(2,1)S(1)}, bf16[2,48,1728]{2,1,0:T(8,128)(2,1)S(1)}, u32[]{:S(2)}, u32[]{:S(2)}) collective-permute-start(bf16[2,48,1728]{2,1,0:T(8,128)(2,1)S(1)} %get-tuple-element.55), channel_id=1, source_target_pairs={{0,4},{4,8},{8,12},{12,0},{1,5},{5,9},{9,13},{13,1},{2,6},{6,10},{... | collective-permute-start | bytes 995336 | tf_op jit(solution)/shard_map/ppermute | solution.py:22
  104.1 24.7 %collective-permute-start.20 = (bf16[4,48,2688]{2,1,0:T(8,128)(2,1)S(1)}, bf16[4,48,2688]{2,1,0:T(8,128)(2,1)S(1)}, u32[]{:S(2)}, u32[]{:S(2)}) collective-permute-start(bf16[4,48,2688]{2,1,0:T(8,128)(2,1)S(1)} %bitcast.111), channel_id=1, source_target_pairs={{0,2},{2,0},{1,3},{3,1},{4,6},{6,4},{5,7},{7,5},{8,10},{10,8},{9,1... | collective-permute-start | bytes 3096584 | tf_op jit(solution)/shard_map/ppermute | solution.py:240
  105.6 10.9 %collective-permute-start.26 = (bf16[2,48,1728]{2,1,0:T(8,128)(2,1)S(1)}, bf16[2,48,1728]{2,1,0:T(8,128)(2,1)S(1)}, u32[]{:S(2)}, u32[]{:S(2)}) collective-permute-start(bf16[2,48,1728]{2,1,0:T(8,128)(2,1)S(1)} %get-tuple-element.56), channel_id=1, source_target_pairs={{0,12},{4,0},{8,4},{12,8},{1,13},{5,1},{9,5},{13,9},{2,14},{6,2},{... | collective-permute-start | bytes 995336 | tf_op jit(solution)/shard_map/ppermute | solution.py:22
  112.2 21.6 %collective-permute-start.25 = (bf16[2,48,3456]{2,1,0:T(8,128)(2,1)S(1)}, bf16[2,48,3456]{2,1,0:T(8,128)(2,1)S(1)}, u32[]{:S(2)}, u32[]{:S(2)}) collective-permute-start(bf16[2,48,3456]{2,1,0:T(8,128)(2,1)S(1)} %pad_maximum_fusion.1), channel_id=1, source_target_pairs={{0,4},{4,8},{8,12},{12,0},{1,5},{5,9},{9,13},{13,1},{2,6},{6,10},{... | collective-permute-start | bytes 1990664 | tf_op jit(solution)/shard_map/ppermute | solution.py:22
  116.8 17.2 %collective-permute-start.27 = (bf16[2,48,3456]{2,1,0:T(8,128)(2,1)S(1)}, bf16[2,48,3456]{2,1,0:T(8,128)(2,1)S(1)}, u32[]{:S(2)}, u32[]{:S(2)}) collective-permute-start(bf16[2,48,3456]{2,1,0:T(8,128)(2,1)S(1)} %pad_maximum_fusion.2), channel_id=1, source_target_pairs={{0,12},{4,0},{8,4},{12,8},{1,13},{5,1},{9,5},{13,9},{2,14},{6,2},{... | collective-permute-start | bytes 1990664 | tf_op jit(solution)/shard_map/ppermute | solution.py:22
  129.1 9.2 %collective-permute-start.21 = (bf16[48,2688]{1,0:T(8,128)(2,1)S(1)}, bf16[48,2688]{1,0:T(8,128)(2,1)S(1)}, u32[]{:S(2)}, u32[]{:S(2)}) collective-permute-start(bf16[48,2688]{1,0:T(8,128)(2,1)S(1)} %get-tuple-element.52), channel_id=1, source_target_pairs={{0,4},{4,8},{8,12},{12,0},{1,5},{5,9},{9,13},{13,1},{2,6},{6,10},{... | collective-permute-start | bytes 774152 | tf_op jit(solution)/shard_map/ppermute | solution.py:22
  130.7 14.0 %collective-permute-start.22 = (bf16[48,2688]{1,0:T(8,128)(2,1)S(1)}, bf16[48,2688]{1,0:T(8,128)(2,1)S(1)}, u32[]{:S(2)}, u32[]{:S(2)}) collective-permute-start(bf16[48,2688]{1,0:T(8,128)(2,1)S(1)} %get-tuple-element.54), channel_id=1, source_target_pairs={{0,12},{4,0},{8,4},{12,8},{1,13},{5,1},{9,5},{13,9},{2,14},{6,2},{... | collective-permute-start | bytes 774152 | tf_op jit(solution)/shard_map/ppermute | solution.py:22
  131.2 13.5 %collective-permute-start.23 = (bf16[48,2688]{1,0:T(8,128)(2,1)S(1)}, bf16[48,2688]{1,0:T(8,128)(2,1)S(1)}, u32[]{:S(2)}, u32[]{:S(2)}) collective-permute-start(bf16[48,2688]{1,0:T(8,128)(2,1)S(1)} %get-tuple-element.53), channel_id=1, source_target_pairs={{0,8},{4,12},{8,0},{12,4},{1,9},{5,13},{9,1},{13,5},{2,10},{6,14},... | collective-permute-start | bytes 774152 | tf_op jit(solution)/shard_map/ppermute | solution.py:22
  134.1 10.7 %collective-permute-start.28 = (bf16[48,3456]{1,0:T(8,128)(2,1)S(1)}, bf16[48,3456]{1,0:T(8,128)(2,1)S(1)}, u32[]{:S(2)}, u32[]{:S(2)}) collective-permute-start(bf16[48,3456]{1,0:T(8,128)(2,1)S(1)} %fusion.5), channel_id=1, source_target_pairs={{0,2},{2,0},{1,3},{3,1},{4,6},{6,4},{5,7},{7,5},{8,10},{10,8},{9,1... | collective-permute-start | bytes 995336 | tf_op jit(solution)/shard_map/ppermute | solution.py:244
  (20 other events, 208.3 us)

commit v3 on v2

--- a/solution.py
+++ b/solution.py
@@ -224,8 +224,8 @@
         return attend(scalars, queries, (0, 1), [keys, values, *lag2])
 
     state, lag1, pieces, scalars = fetch(keys, values, clean_root, z, xh, scalars, first_pass)
+    state = attend(scalars, queries, (2,), [lag1], state)
     state, weight = lax.optimization_barrier((state, weight))
-    state = attend(scalars, queries, (2,), [lag1], state)
     attended = attend(scalars, queries, (3,), pieces, state, last=True)
     taken = lax.ppermute(attended[rows // 2 :], "c", SWAP)
     both = jnp.concatenate([attended[: rows // 2], taken], axis=1)

time: 149 us -> 149 us (level)
  the two profiles are of different devices: /device:TPU:92 before, /device:TPU:24 now
where the time goes in v3:
time: 149 us; the launch traced here: 148 us
  waiting for transfers between devices  51.4 us (34%)
  starting transfers between devices  48.2 us (32%)
  Pallas kernels  14.4 us (10%)
  local copies, waits for them, and re-layouts  13.9 us (9%)
  other arithmetic  10.3 us (7%)
  between operations  5.48 us (4%)
  matrix products  4.29 us (3%)
    ppermute x23, starting transfers between devices, shift(): lax.ppermute(value, axis, [(i, (i + steps) % count) for i in range(count)])  39.6 us
    ppermute x23, waiting for transfers between devices, shift(): lax.ppermute(value, axis, [(i, (i + steps) % count) for i in range(count)])  34.1 us
    pallas_call x3, Pallas kernels, attend(): pl.pallas_call(functools.partial(attend_body, fresh, last, flags), out_sh...  14.4 us
    ppermute x1, waiting for transfers between devices, local(): x_got = lax.ppermute(x_first[1], 'xl', SWAP)  12.2 us
    unnamed x38, local copies, waits for them, and re-layouts  10.5 us
    concatenate x1, other arithmetic, local(): jnp.concatenate([out_weight, lax.ppermute(out_weight, 'c', SWAP)], axis=0)  4.8 us
    dot_general x2, matrix products, project(): jnp.dot(both, weight[:, low:high], preferred_element_type=jnp.float32)  4.29 us
    ppermute x1, waiting for transfers between devices, fetch(): lax.ppermute(piece, 'xh', SWAP)  3.62 us
  transfers between devices with their start and end apart: 29, of which 14 were waited for; matrix products, arithmetic and copies ran while one was open for 10% of the time, Pallas kernels for 6%

profile of v3, /device:TPU:24, one launch (start us, length us, event | category | flops | bytes accessed | tf_op | source)
XLA Modules:
  0.0 148.1 jit_solution(748812198735366286)
XLA Ops:
  1.3 5.9 %collective-permute-start = (bf16[2,96,384]{2,1,0:T(8,128)(2,1)S(1)}, bf16[2,96,384]{2,1,0:T(8,128)(2,1)S(1)}, u32[]{:S(2)}, u32[]{:S(2)}) collective-permute-start(bf16[2,96,384]{2,1,0:T(8,128)(2,1)S(1)} %get-tuple-element.51), channel_id=1, source_target_pairs={{0,224},{32,0},{64,32},{96,64},{128,96},{160,128},{192,160},{224,1... | collective-permute-start | bytes 442376 | tf_op jit(solution)/shard_map/ppermute | solution.py:22
  10.9 3.8 %collective-permute-start.1 = (bf16[2,96,384]{2,1,0:T(8,128)(2,1)S(1)}, bf16[2,96,384]{2,1,0:T(8,128)(2,1)S(1)}, u32[]{:S(2)}, u32[]{:S(2)}) collective-permute-start(bf16[2,96,384]{2,1,0:T(8,128)(2,1)S(1)} %bitcast_select_fusion.4), channel_id=1, source_target_pairs={{0,224},{32,0},{64,32},{96,64},{128,96},{160,128},{192,160},{224,1... | collective-permute-start | bytes 442376 | tf_op jit(solution)/shard_map/ppermute | solution.py:22
  17.6 3.8 %collective-permute-start.2 = (bf16[2,96,384]{2,1,0:T(8,128)(2,1)S(1)}, bf16[2,96,384]{2,1,0:T(8,128)(2,1)S(1)}, u32[]{:S(2)}, u32[]{:S(2)}) collective-permute-start(bf16[2,96,384]{2,1,0:T(8,128)(2,1)S(1)} %bitcast_select_fusion.1), channel_id=1, source_target_pairs={{0,224},{32,0},{64,32},{96,64},{128,96},{160,128},{192,160},{224,1... | collective-permute-start | bytes 442376 | tf_op jit(solution)/shard_map/ppermute | solution.py:22
  21.4 2.7 %collective-permute-done.2 = bf16[2,96,384]{2,1,0:T(8,128)(2,1)S(1)} collective-permute-done((bf16[2,96,384]{2,1,0:T(8,128)(2,1)S(1)}, bf16[2,96,384]{2,1,0:T(8,128)(2,1)S(1)}, u32[]{:S(2)}, u32[]{:S(2)}) %collective-permute-start.2) | collective-permute-done | bytes 147488 | tf_op jit(solution)/shard_map/ppermute | solution.py:22
  24.1 3.8 %collective-permute-start.6 = (bf16[2,96,384]{2,1,0:T(8,128)(2,1)S(1)}, bf16[2,96,384]{2,1,0:T(8,128)(2,1)S(1)}, u32[]{:S(2)}, u32[]{:S(2)}) collective-permute-start(bf16[2,96,384]{2,1,0:T(8,128)(2,1)S(1)} %fusion.17), channel_id=1, source_target_pairs={{0,224},{32,0},{64,32},{96,64},{128,96},{160,128},{192,160},{224,1... | collective-permute-start | bytes 442376 | tf_op jit(solution)/shard_map/ppermute | solution.py:22
  27.9 3.0 %collective-permute-done.4 = bf16[2,96,384]{2,1,0:T(8,128)(2,1)S(1)} collective-permute-done((bf16[2,96,384]{2,1,0:T(8,128)(2,1)S(1)}, bf16[2,96,384]{2,1,0:T(8,128)(2,1)S(1)}, u32[]{:S(2)}, u32[]{:S(2)}) %collective-permute-start.4) | collective-permute-done | bytes 147488 | tf_op jit(solution)/shard_map/ppermute | solution.py:22
  31.3 3.1 %collective-permute-start.7 = (bf16[2,96,384]{2,1,0:T(8,128)(2,1)S(1)}, bf16[2,96,384]{2,1,0:T(8,128)(2,1)S(1)}, u32[]{:S(2)}, u32[]{:S(2)}) collective-permute-start(bf16[2,96,384]{2,1,0:T(8,128)(2,1)S(1)} %get-tuple-element.48), channel_id=1, source_target_pairs={{0,224},{32,0},{64,32},{96,64},{128,96},{160,128},{192,160},{224,1... | collective-permute-start | bytes 442376 | tf_op jit(solution)/shard_map/ppermute | solution.py:22
  34.4 3.0 %collective-permute-done.5 = bf16[2,96,384]{2,1,0:T(8,128)(2,1)S(1)} collective-permute-done((bf16[2,96,384]{2,1,0:T(8,128)(2,1)S(1)}, bf16[2,96,384]{2,1,0:T(8,128)(2,1)S(1)}, u32[]{:S(2)}, u32[]{:S(2)}) %collective-permute-start.5) | collective-permute-done | bytes 147488 | tf_op jit(solution)/shard_map/ppermute | solution.py:22
  37.6 3.1 %collective-permute-start.8 = (bf16[2,96,384]{2,1,0:T(8,128)(2,1)S(1)}, bf16[2,96,384]{2,1,0:T(8,128)(2,1)S(1)}, u32[]{:S(2)}, u32[]{:S(2)}) collective-permute-start(bf16[2,96,384]{2,1,0:T(8,128)(2,1)S(1)} %bitcast_select_fusion.3), channel_id=1, source_target_pairs={{0,16},{16,0},{1,17},{17,1},{2,18},{18,2},{3,19},{19,3},{4,20},{20... | collective-permute-start | bytes 442376 | tf_op jit(solution)/shard_map/ppermute | solution.py:168
  40.8 3.6 %collective-permute-done.8 = bf16[2,96,384]{2,1,0:T(8,128)(2,1)S(1)} collective-permute-done((bf16[2,96,384]{2,1,0:T(8,128)(2,1)S(1)}, bf16[2,96,384]{2,1,0:T(8,128)(2,1)S(1)}, u32[]{:S(2)}, u32[]{:S(2)}) %collective-permute-start.8) | collective-permute-done | bytes 147488 | tf_op jit(solution)/shard_map/ppermute | solution.py:168
  44.4 5.8 %collective-permute-done.9.refs_5_ = bf16[768,384]{1,0:T(8,128)(2,1)S(1)} collective-permute-done((bf16[768,384]{1,0:T(8,128)(2,1)S(1)}, bf16[768,384]{1,0:T(8,128)(2,1)S(1)}, u32[]{:S(2)}, u32[]{:S(2)}) %collective-permute-start.9) | collective-permute-done | bytes 589856 | tf_op jit(solution)/shard_map/ppermute | solution.py:22
  52.4 3.0 %collective-permute-start.17 = (bf16[2,768,384]{2,1,0:T(8,128)(2,1)}, bf16[2,768,384]{2,1,0:T(8,128)(2,1)S(1)}, u32[]{:S(2)}, u32[]{:S(2)}) collective-permute-start(bf16[2,768,384]{2,1,0:T(8,128)(2,1)} %maximum_select_fusion), channel_id=1, source_target_pairs={{0,16},{16,0},{1,17},{17,1},{2,18},{18,2},{3,19},{19,3},{4,20},{20... | collective-permute-start | bytes 3538952 | tf_op jit(solution)/shard_map/ppermute | solution.py:171
  55.4 3.2 %collective-permute-start.11 = (bf16[2,96,384]{2,1,0:T(8,128)(2,1)S(1)}, bf16[2,96,384]{2,1,0:T(8,128)(2,1)}, u32[]{:S(2)}, u32[]{:S(2)}) collective-permute-start(bf16[2,96,384]{2,1,0:T(8,128)(2,1)S(1)} %broadcast_select_fusion.refs_2_), channel_id=1, source_target_pairs={{0,224},{32,0},{64,32},{96,64},{128,96},{160,128},{192,160},{224,1... | collective-permute-start | bytes 442376 | tf_op jit(solution)/shard_map/ppermute | solution.py:22
  60.7 3.7 %shard_map.82 = (f32[3,768,1]{2,1,0:T(8,128)S(1)}, f32[3,768,256]{2,1,0:T(8,128)S(1)}) custom-call(s32[7]{0:T(128)S(1)} %stack.45.refs_0_, bf16[16,48,384]{2,1,0:T(8,128)(2,1)S(1)} %bitcast.102, bf16[768,384]{1,0:T(8,128)(2,1)S(1)} %copy-done.2, bf16[768,384]{1,0:T(8,128)(2,1)S(1)} %copy-done.1, bf16[768,384]{1,0:T(8,128)(2,1)S(1)} %copy-done.9, ...), custom_call_target="tpu_custom_call" | custom-call | flops 1811939328 | bytes 5898240 | tf_op jit(solution)/shard_map/pallas_call | solution.py:135
  70.8 2.9 %collective-permute-done.12.refs_5_ = bf16[2,96,384]{2,1,0:T(8,128)(2,1)S(1)} collective-permute-done((bf16[2,96,384]{2,1,0:T(8,128)(2,1)S(1)}, bf16[2,96,384]{2,1,0:T(8,128)(2,1)S(1)}, u32[]{:S(2)}, u32[]{:S(2)}) %collective-permute-start.12) | collective-permute-done | bytes 147488 | tf_op jit(solution)/shard_map/ppermute | solution.py:22
  77.6 2.5 %collective-permute-start.15 = (bf16[2,96,384]{2,1,0:T(8,128)(2,1)}, bf16[2,96,384]{2,1,0:T(8,128)(2,1)S(1)}, u32[]{:S(2)}, u32[]{:S(2)}) collective-permute-start(bf16[2,96,384]{2,1,0:T(8,128)(2,1)} %collective-permute-done.13.refs_6_), channel_id=1, source_target_pairs={{0,224},{32,0},{64,32},{96,64},{128,96},{160,128},{192,160},{224,1... | collective-permute-start | bytes 442376 | tf_op jit(solution)/shard_map/ppermute | solution.py:22
  83.1 4.8 %shard_map.83 = (f32[3,768,1]{2,1,0:T(8,128)S(1)}, f32[3,768,256]{2,1,0:T(8,128)S(1)}) custom-call(s32[7]{0:T(128)S(1)} %stack.45.refs_0_, bf16[16,48,384]{2,1,0:T(8,128)(2,1)S(1)} %bitcast.103, bf16[2,768,384]{2,1,0:T(8,128)(2,1)S(1)} %collective-permute-done.17.refs_2_, f32[3,768,1]{2,1,0:T(8,128)S(1)} %copy-done.7, f32[3,768,256]{2,1,0:T(8,128)S(1)} %copy-done.5), custom_call_target="tpu_custom_call" | custom-call | flops 905969664 | bytes 5898240 | tf_op jit(solution)/shard_map/pallas_call | solution.py:135
  87.9 4.8 %pad_maximum_fusion = bf16[768,6144]{1,0:T(8,128)(2,1)S(1)} fusion(bf16[384,6144]{1,0:T(8,128)(2,1)} %collective-permute-done.18, bf16[384,6144]{1,0:T(8,128)(2,1)} %param.12), kind=kLoop, calls=%fused_computation | loop fusion | flops 18874368 | bytes 18874368 | tf_op jit(solution)/shard_map/concatenate | solution.py:210
  92.8 5.9 %shard_map.84 = bf16[768,384]{1,0:T(8,128)(2,1)S(1)} custom-call(s32[7]{0:T(128)S(1)} %stack.45.refs_0_, bf16[16,48,384]{2,1,0:T(8,128)(2,1)S(1)} %bitcast.104, bf16[2,96,384]{2,1,0:T(8,128)(2,1)S(1)} %broadcast_select_fusion.refs_2_, bf16[2,96,384]{2,1,0:T(8,128)(2,1)S(1)} %copy-done.13, bf16[2,96,384]{2,1,0:T(8,128)(2,1)} %collective-permute-done.11.refs_4_, ...), custom_call_target="tpu_custom_call" | custom-call | flops 905969664 | bytes 5898240 | tf_op jit(solution)/shard_map/pallas_call | solution.py:135
  108.3 5.2 %collective-permute-done.24 = bf16[2,48,1728]{2,1,0:T(8,128)(2,1)S(1)} collective-permute-done((bf16[2,48,1728]{2,1,0:T(8,128)(2,1)S(1)}, bf16[2,48,1728]{2,1,0:T(8,128)(2,1)S(1)}, u32[]{:S(2)}, u32[]{:S(2)}) %collective-permute-start.24) | collective-permute-done | bytes 331808 | tf_op jit(solution)/shard_map/ppermute | solution.py:22
  118.2 12.2 %collective-permute-done.20 = bf16[4,48,2688]{2,1,0:T(8,128)(2,1)S(1)} collective-permute-done((bf16[4,48,2688]{2,1,0:T(8,128)(2,1)S(1)}, bf16[4,48,2688]{2,1,0:T(8,128)(2,1)S(1)}, u32[]{:S(2)}, u32[]{:S(2)}) %collective-permute-start.20) | collective-permute-done | bytes 1032224 | tf_op jit(solution)/shard_map/ppermute | solution.py:240
  132.9 2.5 %collective-permute-start.23 = (bf16[48,2688]{1,0:T(8,128)(2,1)S(1)}, bf16[48,2688]{1,0:T(8,128)(2,1)S(1)}, u32[]{:S(2)}, u32[]{:S(2)}) collective-permute-start(bf16[48,2688]{1,0:T(8,128)(2,1)S(1)} %get-tuple-element.53), channel_id=1, source_target_pairs={{0,8},{4,12},{8,0},{12,4},{1,9},{5,13},{9,1},{13,5},{2,10},{6,14},... | collective-permute-start | bytes 774152 | tf_op jit(solution)/shard_map/ppermute | solution.py:22
  137.0 3.0 %collective-permute-done.21 = bf16[48,2688]{1,0:T(8,128)(2,1)S(1)} collective-permute-done((bf16[48,2688]{1,0:T(8,128)(2,1)S(1)}, bf16[48,2688]{1,0:T(8,128)(2,1)S(1)}, u32[]{:S(2)}, u32[]{:S(2)}) %collective-permute-start.21) | collective-permute-done | bytes 258080 | tf_op jit(solution)/shard_map/ppermute | solution.py:22
  140.0 5.9 %collective-permute-done.22 = bf16[48,2688]{1,0:T(8,128)(2,1)S(1)} collective-permute-done((bf16[48,2688]{1,0:T(8,128)(2,1)S(1)}, bf16[48,2688]{1,0:T(8,128)(2,1)S(1)}, u32[]{:S(2)}, u32[]{:S(2)}) %collective-permute-start.22) | collective-permute-done | bytes 258080 | tf_op jit(solution)/shard_map/ppermute | solution.py:22
  (107 shorter events, 41.3 us)
Async XLA Ops:
  0.0 87.9 %collective-permute-start.18 = (bf16[384,6144]{1,0:T(8,128)(2,1)}, bf16[384,6144]{1,0:T(8,128)(2,1)}, u32[]{:S(2)}, u32[]{:S(2)}) collective-permute-start(bf16[384,6144]{1,0:T(8,128)(2,1)} %param.12), channel_id=1, source_target_pairs={{0,1},{1,0},{2,3},{3,2},{4,5},{5,4},{6,7},{7,6},{8,9},{9,8},{10,11... | collective-permute-start | bytes 14155784 | tf_op jit(solution)/shard_map/ppermute | solution.py:210
  1.3 9.6 %collective-permute-start = (bf16[2,96,384]{2,1,0:T(8,128)(2,1)S(1)}, bf16[2,96,384]{2,1,0:T(8,128)(2,1)S(1)}, u32[]{:S(2)}, u32[]{:S(2)}) collective-permute-start(bf16[2,96,384]{2,1,0:T(8,128)(2,1)S(1)} %get-tuple-element.51), channel_id=1, source_target_pairs={{0,224},{32,0},{64,32},{96,64},{128,96},{160,128},{192,160},{224,1... | collective-permute-start | bytes 442376 | tf_op jit(solution)/shard_map/ppermute | solution.py:22
  7.2 16.9 %collective-permute-start.3 = (bf16[768,384]{1,0:T(8,128)(2,1)S(1)}, bf16[768,384]{1,0:T(8,128)(2,1)S(1)}, u32[]{:S(2)}, u32[]{:S(2)}) collective-permute-start(bf16[768,384]{1,0:T(8,128)(2,1)S(1)} %copy-done.2), channel_id=1, source_target_pairs={{0,32},{32,64},{64,96},{96,128},{128,160},{160,192},{192,224},{224... | collective-permute-start | bytes 1769480 | tf_op jit(solution)/shard_map/ppermute | solution.py:22
  10.9 6.7 %collective-permute-start.1 = (bf16[2,96,384]{2,1,0:T(8,128)(2,1)S(1)}, bf16[2,96,384]{2,1,0:T(8,128)(2,1)S(1)}, u32[]{:S(2)}, u32[]{:S(2)}) collective-permute-start(bf16[2,96,384]{2,1,0:T(8,128)(2,1)S(1)} %bitcast_select_fusion.4), channel_id=1, source_target_pairs={{0,224},{32,0},{64,32},{96,64},{128,96},{160,128},{192,160},{224,1... | collective-permute-start | bytes 442376 | tf_op jit(solution)/shard_map/ppermute | solution.py:22
  24.1 6.8 %collective-permute-start.4 = (bf16[2,96,384]{2,1,0:T(8,128)(2,1)S(1)}, bf16[2,96,384]{2,1,0:T(8,128)(2,1)S(1)}, u32[]{:S(2)}, u32[]{:S(2)}) collective-permute-start(bf16[2,96,384]{2,1,0:T(8,128)(2,1)S(1)} %get-tuple-element.27), channel_id=1, source_target_pairs={{0,32},{32,64},{64,96},{96,128},{128,160},{160,192},{192,224},{224... | collective-permute-start | bytes 442376 | tf_op jit(solution)/shard_map/ppermute | solution.py:22
  24.1 6.8 %collective-permute-start.6 = (bf16[2,96,384]{2,1,0:T(8,128)(2,1)S(1)}, bf16[2,96,384]{2,1,0:T(8,128)(2,1)S(1)}, u32[]{:S(2)}, u32[]{:S(2)}) collective-permute-start(bf16[2,96,384]{2,1,0:T(8,128)(2,1)S(1)} %fusion.17), channel_id=1, source_target_pairs={{0,224},{32,0},{64,32},{96,64},{128,96},{160,128},{192,160},{224,1... | collective-permute-start | bytes 442376 | tf_op jit(solution)/shard_map/ppermute | solution.py:22
  37.5 12.7 %collective-permute-start.9 = (bf16[768,384]{1,0:T(8,128)(2,1)S(1)}, bf16[768,384]{1,0:T(8,128)(2,1)S(1)}, u32[]{:S(2)}, u32[]{:S(2)}) collective-permute-start(bf16[768,384]{1,0:T(8,128)(2,1)S(1)} %copy-done.1), channel_id=1, source_target_pairs={{0,32},{32,64},{64,96},{96,128},{128,160},{160,192},{192,224},{224... | collective-permute-start | bytes 1769480 | tf_op jit(solution)/shard_map/ppermute | solution.py:22
  37.6 6.7 %collective-permute-start.8 = (bf16[2,96,384]{2,1,0:T(8,128)(2,1)S(1)}, bf16[2,96,384]{2,1,0:T(8,128)(2,1)S(1)}, u32[]{:S(2)}, u32[]{:S(2)}) collective-permute-start(bf16[2,96,384]{2,1,0:T(8,128)(2,1)S(1)} %bitcast_select_fusion.3), channel_id=1, source_target_pairs={{0,16},{16,0},{1,17},{17,1},{2,18},{18,2},{3,19},{19,3},{4,20},{20... | collective-permute-start | bytes 442376 | tf_op jit(solution)/shard_map/ppermute | solution.py:168
  52.4 27.8 %collective-permute-start.17 = (bf16[2,768,384]{2,1,0:T(8,128)(2,1)}, bf16[2,768,384]{2,1,0:T(8,128)(2,1)S(1)}, u32[]{:S(2)}, u32[]{:S(2)}) collective-permute-start(bf16[2,768,384]{2,1,0:T(8,128)(2,1)} %maximum_select_fusion), channel_id=1, source_target_pairs={{0,16},{16,0},{1,17},{17,1},{2,18},{18,2},{3,19},{19,3},{4,20},{20... | collective-permute-start | bytes 3538952 | tf_op jit(solution)/shard_map/ppermute | solution.py:171
  55.4 11.5 %collective-permute-start.10 = (bf16[2,96,384]{2,1,0:T(8,128)(2,1)S(1)}, bf16[2,96,384]{2,1,0:T(8,128)(2,1)S(1)}, u32[]{:S(2)}, u32[]{:S(2)}) collective-permute-start(bf16[2,96,384]{2,1,0:T(8,128)(2,1)S(1)} %broadcast_select_fusion.refs_2_), channel_id=1, source_target_pairs={{0,32},{32,64},{64,96},{96,128},{128,160},{160,192},{192,224},{224... | collective-permute-start | bytes 442376 | tf_op jit(solution)/shard_map/ppermute | solution.py:22
  55.4 14.6 %collective-permute-start.11 = (bf16[2,96,384]{2,1,0:T(8,128)(2,1)S(1)}, bf16[2,96,384]{2,1,0:T(8,128)(2,1)}, u32[]{:S(2)}, u32[]{:S(2)}) collective-permute-start(bf16[2,96,384]{2,1,0:T(8,128)(2,1)S(1)} %broadcast_select_fusion.refs_2_), channel_id=1, source_target_pairs={{0,224},{32,0},{64,32},{96,64},{128,96},{160,128},{192,160},{224,1... | collective-permute-start | bytes 442376 | tf_op jit(solution)/shard_map/ppermute | solution.py:22
  66.9 6.8 %collective-permute-start.12 = (bf16[2,96,384]{2,1,0:T(8,128)(2,1)S(1)}, bf16[2,96,384]{2,1,0:T(8,128)(2,1)S(1)}, u32[]{:S(2)}, u32[]{:S(2)}) collective-permute-start(bf16[2,96,384]{2,1,0:T(8,128)(2,1)S(1)} %collective-permute-done.10.refs_3_), channel_id=1, source_target_pairs={{0,32},{32,64},{64,96},{96,128},{128,160},{160,192},{192,224},{224... | collective-permute-start | bytes 442376 | tf_op jit(solution)/shard_map/ppermute | solution.py:22
  70.0 7.6 %collective-permute-start.13 = (bf16[2,96,384]{2,1,0:T(8,128)(2,1)}, bf16[2,96,384]{2,1,0:T(8,128)(2,1)}, u32[]{:S(2)}, u32[]{:S(2)}) collective-permute-start(bf16[2,96,384]{2,1,0:T(8,128)(2,1)} %collective-permute-done.11.refs_4_), channel_id=1, source_target_pairs={{0,224},{32,0},{64,32},{96,64},{128,96},{160,128},{192,160},{224,1... | collective-permute-start | bytes 442376 | tf_op jit(solution)/shard_map/ppermute | solution.py:22
  77.6 15.2 %collective-permute-start.15 = (bf16[2,96,384]{2,1,0:T(8,128)(2,1)}, bf16[2,96,384]{2,1,0:T(8,128)(2,1)S(1)}, u32[]{:S(2)}, u32[]{:S(2)}) collective-permute-start(bf16[2,96,384]{2,1,0:T(8,128)(2,1)} %collective-permute-done.13.refs_6_), channel_id=1, source_target_pairs={{0,224},{32,0},{64,32},{96,64},{128,96},{160,128},{192,160},{224,1... | collective-permute-start | bytes 442376 | tf_op jit(solution)/shard_map/ppermute | solution.py:22
  80.1 12.7 %collective-permute-start.16 = (bf16[2,96,384]{2,1,0:T(8,128)(2,1)}, bf16[2,96,384]{2,1,0:T(8,128)(2,1)S(1)}, u32[]{:S(2)}, u32[]{:S(2)}) collective-permute-start(bf16[2,96,384]{2,1,0:T(8,128)(2,1)} %collective-permute-done.14.refs_7_), channel_id=1, source_target_pairs={{0,32},{32,64},{64,96},{96,128},{128,160},{160,192},{192,224},{224... | collective-permute-start | bytes 442376 | tf_op jit(solution)/shard_map/ppermute | solution.py:22
  103.3 10.2 %collective-permute-start.24 = (bf16[2,48,1728]{2,1,0:T(8,128)(2,1)S(1)}, bf16[2,48,1728]{2,1,0:T(8,128)(2,1)S(1)}, u32[]{:S(2)}, u32[]{:S(2)}) collective-permute-start(bf16[2,48,1728]{2,1,0:T(8,128)(2,1)S(1)} %get-tuple-element.55), channel_id=1, source_target_pairs={{0,4},{4,8},{8,12},{12,0},{1,5},{5,9},{9,13},{13,1},{2,6},{6,10},{... | collective-permute-start | bytes 995336 | tf_op jit(solution)/shard_map/ppermute | solution.py:22
  105.7 24.7 %collective-permute-start.20 = (bf16[4,48,2688]{2,1,0:T(8,128)(2,1)S(1)}, bf16[4,48,2688]{2,1,0:T(8,128)(2,1)S(1)}, u32[]{:S(2)}, u32[]{:S(2)}) collective-permute-start(bf16[4,48,2688]{2,1,0:T(8,128)(2,1)S(1)} %bitcast.111), channel_id=1, source_target_pairs={{0,2},{2,0},{1,3},{3,1},{4,6},{6,4},{5,7},{7,5},{8,10},{10,8},{9,1... | collective-permute-start | bytes 3096584 | tf_op jit(solution)/shard_map/ppermute | solution.py:240
  106.4 10.9 %collective-permute-start.26 = (bf16[2,48,1728]{2,1,0:T(8,128)(2,1)S(1)}, bf16[2,48,1728]{2,1,0:T(8,128)(2,1)S(1)}, u32[]{:S(2)}, u32[]{:S(2)}) collective-permute-start(bf16[2,48,1728]{2,1,0:T(8,128)(2,1)S(1)} %get-tuple-element.56), channel_id=1, source_target_pairs={{0,12},{4,0},{8,4},{12,8},{1,13},{5,1},{9,5},{13,9},{2,14},{6,2},{... | collective-permute-start | bytes 995336 | tf_op jit(solution)/shard_map/ppermute | solution.py:22
  113.8 21.6 %collective-permute-start.25 = (bf16[2,48,3456]{2,1,0:T(8,128)(2,1)S(1)}, bf16[2,48,3456]{2,1,0:T(8,128)(2,1)S(1)}, u32[]{:S(2)}, u32[]{:S(2)}) collective-permute-start(bf16[2,48,3456]{2,1,0:T(8,128)(2,1)S(1)} %pad_maximum_fusion.1), channel_id=1, source_target_pairs={{0,4},{4,8},{8,12},{12,0},{1,5},{5,9},{9,13},{13,1},{2,6},{6,10},{... | collective-permute-start | bytes 1990664 | tf_op jit(solution)/shard_map/ppermute | solution.py:22
  117.6 17.7 %collective-permute-start.27 = (bf16[2,48,3456]{2,1,0:T(8,128)(2,1)S(1)}, bf16[2,48,3456]{2,1,0:T(8,128)(2,1)S(1)}, u32[]{:S(2)}, u32[]{:S(2)}) collective-permute-start(bf16[2,48,3456]{2,1,0:T(8,128)(2,1)S(1)} %pad_maximum_fusion.2), channel_id=1, source_target_pairs={{0,12},{4,0},{8,4},{12,8},{1,13},{5,1},{9,5},{13,9},{2,14},{6,2},{... | collective-permute-start | bytes 1990664 | tf_op jit(solution)/shard_map/ppermute | solution.py:22
  130.7 9.2 %collective-permute-start.21 = (bf16[48,2688]{1,0:T(8,128)(2,1)S(1)}, bf16[48,2688]{1,0:T(8,128)(2,1)S(1)}, u32[]{:S(2)}, u32[]{:S(2)}) collective-permute-start(bf16[48,2688]{1,0:T(8,128)(2,1)S(1)} %get-tuple-element.52), channel_id=1, source_target_pairs={{0,4},{4,8},{8,12},{12,0},{1,5},{5,9},{9,13},{13,1},{2,6},{6,10},{... | collective-permute-start | bytes 774152 | tf_op jit(solution)/shard_map/ppermute | solution.py:22
  132.3 13.6 %collective-permute-start.22 = (bf16[48,2688]{1,0:T(8,128)(2,1)S(1)}, bf16[48,2688]{1,0:T(8,128)(2,1)S(1)}, u32[]{:S(2)}, u32[]{:S(2)}) collective-permute-start(bf16[48,2688]{1,0:T(8,128)(2,1)S(1)} %get-tuple-element.54), channel_id=1, source_target_pairs={{0,12},{4,0},{8,4},{12,8},{1,13},{5,1},{9,5},{13,9},{2,14},{6,2},{... | collective-permute-start | bytes 774152 | tf_op jit(solution)/shard_map/ppermute | solution.py:22
  132.9 13.0 %collective-permute-start.23 = (bf16[48,2688]{1,0:T(8,128)(2,1)S(1)}, bf16[48,2688]{1,0:T(8,128)(2,1)S(1)}, u32[]{:S(2)}, u32[]{:S(2)}) collective-permute-start(bf16[48,2688]{1,0:T(8,128)(2,1)S(1)} %get-tuple-element.53), channel_id=1, source_target_pairs={{0,8},{4,12},{8,0},{12,4},{1,9},{5,13},{9,1},{13,5},{2,10},{6,14},... | collective-permute-start | bytes 774152 | tf_op jit(solution)/shard_map/ppermute | solution.py:22
  135.5 10.5 %collective-permute-start.28 = (bf16[48,3456]{1,0:T(8,128)(2,1)S(1)}, bf16[48,3456]{1,0:T(8,128)(2,1)S(1)}, u32[]{:S(2)}, u32[]{:S(2)}) collective-permute-start(bf16[48,3456]{1,0:T(8,128)(2,1)S(1)} %fusion.5), channel_id=1, source_target_pairs={{0,2},{2,0},{1,3},{3,1},{4,6},{6,4},{5,7},{7,5},{8,10},{10,8},{9,1... | collective-permute-start | bytes 995336 | tf_op jit(solution)/shard_map/ppermute | solution.py:244
  (24 other events, 222.1 us)

commit v4 on v2

--- a/solution.py
+++ b/solution.py
@@ -175,6 +175,8 @@
     for number in range(4):
         if number == 1:
             up, peak = lax.optimization_barrier((up, peak))
+        if number == 3:
+            up, lag1 = lax.optimization_barrier((up, lag1))
         up = shift(up, "z", NZ, 1)
         pieces.append(up)
         if number < 3:

time: 149 us -> 148 us (level)
  the two profiles are of different devices: /device:TPU:92 before, /device:TPU:24 now
where the time goes in v4:
time: 148 us; the launch traced here: 149 us
  waiting for transfers between devices  52 us (35%)
  starting transfers between devices  48.2 us (33%)
  Pallas kernels  18.1 us (12%)
  local copies, waits for them, and re-layouts  10.4 us (7%)
  other arithmetic  10.4 us (7%)
  between operations  5.51 us (4%)
  matrix products  4.29 us (3%)
    ppermute x23, starting transfers between devices, shift(): lax.ppermute(value, axis, [(i, (i + steps) % count) for i in range(count)])  39.6 us
    ppermute x23, waiting for transfers between devices, shift(): lax.ppermute(value, axis, [(i, (i + steps) % count) for i in range(count)])  34.7 us
    pallas_call x3, Pallas kernels, attend(): pl.pallas_call(functools.partial(attend_body, fresh, last, flags), out_sh...  18.1 us
    ppermute x1, waiting for transfers between devices, local(): x_got = lax.ppermute(x_first[1], 'xl', SWAP)  12.2 us
    unnamed x38, local copies, waits for them, and re-layouts  6.92 us
    concatenate x1, other arithmetic, local(): jnp.concatenate([out_weight, lax.ppermute(out_weight, 'c', SWAP)], axis=0)  4.93 us
    dot_general x2, matrix products, project(): jnp.dot(both, weight[:, low:high], preferred_element_type=jnp.float32)  4.29 us
    ppermute x1, waiting for transfers between devices, fetch(): lax.ppermute(piece, 'xh', SWAP)  3.62 us
  transfers between devices with their start and end apart: 29, of which 15 were waited for; matrix products, arithmetic and copies ran while one was open for 10% of the time, Pallas kernels for 8%

profile of v4, /device:TPU:24, one launch (start us, length us, event | category | flops | bytes accessed | tf_op | source)
XLA Modules:
  0.0 148.9 jit_solution(654918366346359099)
XLA Ops:
  1.3 5.9 %collective-permute-start = (bf16[2,96,384]{2,1,0:T(8,128)(2,1)S(1)}, bf16[2,96,384]{2,1,0:T(8,128)(2,1)S(1)}, u32[]{:S(2)}, u32[]{:S(2)}) collective-permute-start(bf16[2,96,384]{2,1,0:T(8,128)(2,1)S(1)} %get-tuple-element.54), channel_id=1, source_target_pairs={{0,224},{32,0},{64,32},{96,64},{128,96},{160,128},{192,160},{224,1... | collective-permute-start | bytes 442376 | tf_op jit(solution)/shard_map/ppermute | solution.py:22
  10.9 3.8 %collective-permute-start.1 = (bf16[2,96,384]{2,1,0:T(8,128)(2,1)S(1)}, bf16[2,96,384]{2,1,0:T(8,128)(2,1)S(1)}, u32[]{:S(2)}, u32[]{:S(2)}) collective-permute-start(bf16[2,96,384]{2,1,0:T(8,128)(2,1)S(1)} %bitcast_select_fusion.4), channel_id=1, source_target_pairs={{0,224},{32,0},{64,32},{96,64},{128,96},{160,128},{192,160},{224,1... | collective-permute-start | bytes 442376 | tf_op jit(solution)/shard_map/ppermute | solution.py:22
  17.6 3.8 %collective-permute-start.2 = (bf16[2,96,384]{2,1,0:T(8,128)(2,1)S(1)}, bf16[2,96,384]{2,1,0:T(8,128)(2,1)S(1)}, u32[]{:S(2)}, u32[]{:S(2)}) collective-permute-start(bf16[2,96,384]{2,1,0:T(8,128)(2,1)S(1)} %bitcast_select_fusion.1), channel_id=1, source_target_pairs={{0,224},{32,0},{64,32},{96,64},{128,96},{160,128},{192,160},{224,1... | collective-permute-start | bytes 442376 | tf_op jit(solution)/shard_map/ppermute | solution.py:22
  21.4 2.7 %collective-permute-done.2 = bf16[2,96,384]{2,1,0:T(8,128)(2,1)S(1)} collective-permute-done((bf16[2,96,384]{2,1,0:T(8,128)(2,1)S(1)}, bf16[2,96,384]{2,1,0:T(8,128)(2,1)S(1)}, u32[]{:S(2)}, u32[]{:S(2)}) %collective-permute-start.2) | collective-permute-done | bytes 147488 | tf_op jit(solution)/shard_map/ppermute | solution.py:22
  24.1 3.8 %collective-permute-start.6 = (bf16[2,96,384]{2,1,0:T(8,128)(2,1)S(1)}, bf16[2,96,384]{2,1,0:T(8,128)(2,1)S(1)}, u32[]{:S(2)}, u32[]{:S(2)}) collective-permute-start(bf16[2,96,384]{2,1,0:T(8,128)(2,1)S(1)} %fusion.17), channel_id=1, source_target_pairs={{0,224},{32,0},{64,32},{96,64},{128,96},{160,128},{192,160},{224,1... | collective-permute-start | bytes 442376 | tf_op jit(solution)/shard_map/ppermute | solution.py:22
  27.9 3.0 %collective-permute-done.4 = bf16[2,96,384]{2,1,0:T(8,128)(2,1)S(1)} collective-permute-done((bf16[2,96,384]{2,1,0:T(8,128)(2,1)S(1)}, bf16[2,96,384]{2,1,0:T(8,128)(2,1)S(1)}, u32[]{:S(2)}, u32[]{:S(2)}) %collective-permute-start.4) | collective-permute-done | bytes 147488 | tf_op jit(solution)/shard_map/ppermute | solution.py:22
  31.3 3.1 %collective-permute-start.7 = (bf16[2,96,384]{2,1,0:T(8,128)(2,1)S(1)}, bf16[2,96,384]{2,1,0:T(8,128)(2,1)S(1)}, u32[]{:S(2)}, u32[]{:S(2)}) collective-permute-start(bf16[2,96,384]{2,1,0:T(8,128)(2,1)S(1)} %get-tuple-element.52), channel_id=1, source_target_pairs={{0,224},{32,0},{64,32},{96,64},{128,96},{160,128},{192,160},{224,1... | collective-permute-start | bytes 442376 | tf_op jit(solution)/shard_map/ppermute | solution.py:22
  34.4 3.0 %collective-permute-done.5 = bf16[2,96,384]{2,1,0:T(8,128)(2,1)S(1)} collective-permute-done((bf16[2,96,384]{2,1,0:T(8,128)(2,1)S(1)}, bf16[2,96,384]{2,1,0:T(8,128)(2,1)S(1)}, u32[]{:S(2)}, u32[]{:S(2)}) %collective-permute-start.5) | collective-permute-done | bytes 147488 | tf_op jit(solution)/shard_map/ppermute | solution.py:22
  37.6 3.1 %collective-permute-start.8 = (bf16[2,96,384]{2,1,0:T(8,128)(2,1)S(1)}, bf16[2,96,384]{2,1,0:T(8,128)(2,1)S(1)}, u32[]{:S(2)}, u32[]{:S(2)}) collective-permute-start(bf16[2,96,384]{2,1,0:T(8,128)(2,1)S(1)} %bitcast_select_fusion.3), channel_id=1, source_target_pairs={{0,16},{16,0},{1,17},{17,1},{2,18},{18,2},{3,19},{19,3},{4,20},{20... | collective-permute-start | bytes 442376 | tf_op jit(solution)/shard_map/ppermute | solution.py:168
  40.8 3.6 %collective-permute-done.8 = bf16[2,96,384]{2,1,0:T(8,128)(2,1)S(1)} collective-permute-done((bf16[2,96,384]{2,1,0:T(8,128)(2,1)S(1)}, bf16[2,96,384]{2,1,0:T(8,128)(2,1)S(1)}, u32[]{:S(2)}, u32[]{:S(2)}) %collective-permute-start.8) | collective-permute-done | bytes 147488 | tf_op jit(solution)/shard_map/ppermute | solution.py:168
  44.4 5.8 %collective-permute-done.9.refs_5_ = bf16[768,384]{1,0:T(8,128)(2,1)S(1)} collective-permute-done((bf16[768,384]{1,0:T(8,128)(2,1)S(1)}, bf16[768,384]{1,0:T(8,128)(2,1)S(1)}, u32[]{:S(2)}, u32[]{:S(2)}) %collective-permute-start.9) | collective-permute-done | bytes 589856 | tf_op jit(solution)/shard_map/ppermute | solution.py:22
  52.4 3.0 %collective-permute-start.16 = (bf16[2,768,384]{2,1,0:T(8,128)(2,1)}, bf16[2,768,384]{2,1,0:T(8,128)(2,1)S(1)}, u32[]{:S(2)}, u32[]{:S(2)}) collective-permute-start(bf16[2,768,384]{2,1,0:T(8,128)(2,1)} %maximum_select_fusion), channel_id=1, source_target_pairs={{0,16},{16,0},{1,17},{17,1},{2,18},{18,2},{3,19},{19,3},{4,20},{20... | collective-permute-start | bytes 3538952 | tf_op jit(solution)/shard_map/ppermute | solution.py:171
  55.4 3.2 %collective-permute-start.11 = (bf16[2,96,384]{2,1,0:T(8,128)(2,1)S(1)}, bf16[2,96,384]{2,1,0:T(8,128)(2,1)}, u32[]{:S(2)}, u32[]{:S(2)}) collective-permute-start(bf16[2,96,384]{2,1,0:T(8,128)(2,1)S(1)} %broadcast_select_fusion.refs_2_), channel_id=1, source_target_pairs={{0,224},{32,0},{64,32},{96,64},{128,96},{160,128},{192,160},{224,1... | collective-permute-start | bytes 442376 | tf_op jit(solution)/shard_map/ppermute | solution.py:22
  60.7 7.4 %shard_map.82 = (f32[3,768,1]{2,1,0:T(8,128)S(1)}, f32[3,768,256]{2,1,0:T(8,128)S(1)}) custom-call(s32[7]{0:T(128)S(1)} %stack.45.refs_0_, bf16[16,48,384]{2,1,0:T(8,128)(2,1)S(1)} %bitcast.102, bf16[768,384]{1,0:T(8,128)(2,1)S(1)} %copy-done.2, bf16[768,384]{1,0:T(8,128)(2,1)S(1)} %copy-done.1, bf16[768,384]{1,0:T(8,128)(2,1)S(1)} %copy-done.9, ...), custom_call_target="tpu_custom_call" | custom-call | flops 1811939328 | bytes 5898240 | tf_op jit(solution)/shard_map/pallas_call | solution.py:135
  71.2 3.2 %collective-permute-start.13 = (bf16[2,96,384]{2,1,0:T(8,128)(2,1)}, bf16[2,96,384]{2,1,0:T(8,128)(2,1)}, u32[]{:S(2)}, u32[]{:S(2)}) collective-permute-start(bf16[2,96,384]{2,1,0:T(8,128)(2,1)} %collective-permute-done.11.refs_4_), channel_id=1, source_target_pairs={{0,224},{32,0},{64,32},{96,64},{128,96},{160,128},{192,160},{224,1... | collective-permute-start | bytes 442376 | tf_op jit(solution)/shard_map/ppermute | solution.py:22
  74.4 2.9 %collective-permute-done.12.refs_5_ = bf16[2,96,384]{2,1,0:T(8,128)(2,1)S(1)} collective-permute-done((bf16[2,96,384]{2,1,0:T(8,128)(2,1)S(1)}, bf16[2,96,384]{2,1,0:T(8,128)(2,1)S(1)}, u32[]{:S(2)}, u32[]{:S(2)}) %collective-permute-start.12) | collective-permute-done | bytes 147488 | tf_op jit(solution)/shard_map/ppermute | solution.py:22
  79.8 3.3 %collective-permute-start.15 = (bf16[2,96,384]{2,1,0:T(8,128)(2,1)}, bf16[2,96,384]{2,1,0:T(8,128)(2,1)S(1)}, u32[]{:S(2)}, u32[]{:S(2)}) collective-permute-start(bf16[2,96,384]{2,1,0:T(8,128)(2,1)} %collective-permute-done.13.refs_6_), channel_id=1, source_target_pairs={{0,224},{32,0},{64,32},{96,64},{128,96},{160,128},{192,160},{224,1... | collective-permute-start | bytes 442376 | tf_op jit(solution)/shard_map/ppermute | solution.py:22
  83.8 4.9 %pad_maximum_fusion = bf16[768,6144]{1,0:T(8,128)(2,1)S(1)} fusion(bf16[384,6144]{1,0:T(8,128)(2,1)} %collective-permute-done.18, bf16[384,6144]{1,0:T(8,128)(2,1)} %param.12), kind=kLoop, calls=%fused_computation | loop fusion | flops 18874368 | bytes 18874368 | tf_op jit(solution)/shard_map/concatenate | solution.py:212
  88.8 4.8 %shard_map.83 = (f32[3,768,1]{2,1,0:T(8,128)S(1)}, f32[3,768,256]{2,1,0:T(8,128)S(1)}) custom-call(s32[7]{0:T(128)S(1)} %stack.45.refs_0_, bf16[16,48,384]{2,1,0:T(8,128)(2,1)S(1)} %bitcast.103, bf16[2,768,384]{2,1,0:T(8,128)(2,1)S(1)} %collective-permute-done.16.refs_2_, f32[3,768,1]{2,1,0:T(8,128)S(1)} %copy-done.7, f32[3,768,256]{2,1,0:T(8,128)S(1)} %copy-done.5), custom_call_target="tpu_custom_call" | custom-call | flops 905969664 | bytes 5898240 | tf_op jit(solution)/shard_map/pallas_call | solution.py:135
  93.7 5.9 %shard_map.84 = bf16[768,384]{1,0:T(8,128)(2,1)S(1)} custom-call(s32[7]{0:T(128)S(1)} %stack.45.refs_0_, bf16[16,48,384]{2,1,0:T(8,128)(2,1)S(1)} %bitcast.104, bf16[2,96,384]{2,1,0:T(8,128)(2,1)S(1)} %broadcast_select_fusion.refs_2_, bf16[2,96,384]{2,1,0:T(8,128)(2,1)S(1)} %copy-done.13, bf16[2,96,384]{2,1,0:T(8,128)(2,1)} %collective-permute-done.11.refs_4_, ...), custom_call_target="tpu_custom_call" | custom-call | flops 905969664 | bytes 5898240 | tf_op jit(solution)/shard_map/pallas_call | solution.py:135
  109.2 5.2 %collective-permute-done.24 = bf16[2,48,1728]{2,1,0:T(8,128)(2,1)S(1)} collective-permute-done((bf16[2,48,1728]{2,1,0:T(8,128)(2,1)S(1)}, bf16[2,48,1728]{2,1,0:T(8,128)(2,1)S(1)}, u32[]{:S(2)}, u32[]{:S(2)}) %collective-permute-start.24) | collective-permute-done | bytes 331808 | tf_op jit(solution)/shard_map/ppermute | solution.py:22
  119.1 12.2 %collective-permute-done.20 = bf16[4,48,2688]{2,1,0:T(8,128)(2,1)S(1)} collective-permute-done((bf16[4,48,2688]{2,1,0:T(8,128)(2,1)S(1)}, bf16[4,48,2688]{2,1,0:T(8,128)(2,1)S(1)}, u32[]{:S(2)}, u32[]{:S(2)}) %collective-permute-start.20) | collective-permute-done | bytes 1032224 | tf_op jit(solution)/shard_map/ppermute | solution.py:242
  137.9 3.0 %collective-permute-done.21 = bf16[48,2688]{1,0:T(8,128)(2,1)S(1)} collective-permute-done((bf16[48,2688]{1,0:T(8,128)(2,1)S(1)}, bf16[48,2688]{1,0:T(8,128)(2,1)S(1)}, u32[]{:S(2)}, u32[]{:S(2)}) %collective-permute-start.21) | collective-permute-done | bytes 258080 | tf_op jit(solution)/shard_map/ppermute | solution.py:22
  140.9 5.9 %collective-permute-done.22 = bf16[48,2688]{1,0:T(8,128)(2,1)S(1)} collective-permute-done((bf16[48,2688]{1,0:T(8,128)(2,1)S(1)}, bf16[48,2688]{1,0:T(8,128)(2,1)S(1)}, u32[]{:S(2)}, u32[]{:S(2)}) %collective-permute-start.22) | collective-permute-done | bytes 258080 | tf_op jit(solution)/shard_map/ppermute | solution.py:22
  (107 shorter events, 36.9 us)
Async XLA Ops:
  0.0 83.7 %collective-permute-start.18 = (bf16[384,6144]{1,0:T(8,128)(2,1)}, bf16[384,6144]{1,0:T(8,128)(2,1)}, u32[]{:S(2)}, u32[]{:S(2)}) collective-permute-start(bf16[384,6144]{1,0:T(8,128)(2,1)} %param.12), channel_id=1, source_target_pairs={{0,1},{1,0},{2,3},{3,2},{4,5},{5,4},{6,7},{7,6},{8,9},{9,8},{10,11... | collective-permute-start | bytes 14155784 | tf_op jit(solution)/shard_map/ppermute | solution.py:212
  1.3 9.6 %collective-permute-start = (bf16[2,96,384]{2,1,0:T(8,128)(2,1)S(1)}, bf16[2,96,384]{2,1,0:T(8,128)(2,1)S(1)}, u32[]{:S(2)}, u32[]{:S(2)}) collective-permute-start(bf16[2,96,384]{2,1,0:T(8,128)(2,1)S(1)} %get-tuple-element.54), channel_id=1, source_target_pairs={{0,224},{32,0},{64,32},{96,64},{128,96},{160,128},{192,160},{224,1... | collective-permute-start | bytes 442376 | tf_op jit(solution)/shard_map/ppermute | solution.py:22
  7.2 16.9 %collective-permute-start.3 = (bf16[768,384]{1,0:T(8,128)(2,1)S(1)}, bf16[768,384]{1,0:T(8,128)(2,1)S(1)}, u32[]{:S(2)}, u32[]{:S(2)}) collective-permute-start(bf16[768,384]{1,0:T(8,128)(2,1)S(1)} %copy-done.2), channel_id=1, source_target_pairs={{0,32},{32,64},{64,96},{96,128},{128,160},{160,192},{192,224},{224... | collective-permute-start | bytes 1769480 | tf_op jit(solution)/shard_map/ppermute | solution.py:22
  10.9 6.7 %collective-permute-start.1 = (bf16[2,96,384]{2,1,0:T(8,128)(2,1)S(1)}, bf16[2,96,384]{2,1,0:T(8,128)(2,1)S(1)}, u32[]{:S(2)}, u32[]{:S(2)}) collective-permute-start(bf16[2,96,384]{2,1,0:T(8,128)(2,1)S(1)} %bitcast_select_fusion.4), channel_id=1, source_target_pairs={{0,224},{32,0},{64,32},{96,64},{128,96},{160,128},{192,160},{224,1... | collective-permute-start | bytes 442376 | tf_op jit(solution)/shard_map/ppermute | solution.py:22
  24.1 6.8 %collective-permute-start.4 = (bf16[2,96,384]{2,1,0:T(8,128)(2,1)S(1)}, bf16[2,96,384]{2,1,0:T(8,128)(2,1)S(1)}, u32[]{:S(2)}, u32[]{:S(2)}) collective-permute-start(bf16[2,96,384]{2,1,0:T(8,128)(2,1)S(1)} %get-tuple-element.29), channel_id=1, source_target_pairs={{0,32},{32,64},{64,96},{96,128},{128,160},{160,192},{192,224},{224... | collective-permute-start | bytes 442376 | tf_op jit(solution)/shard_map/ppermute | solution.py:22
  24.1 6.8 %collective-permute-start.6 = (bf16[2,96,384]{2,1,0:T(8,128)(2,1)S(1)}, bf16[2,96,384]{2,1,0:T(8,128)(2,1)S(1)}, u32[]{:S(2)}, u32[]{:S(2)}) collective-permute-start(bf16[2,96,384]{2,1,0:T(8,128)(2,1)S(1)} %fusion.17), channel_id=1, source_target_pairs={{0,224},{32,0},{64,32},{96,64},{128,96},{160,128},{192,160},{224,1... | collective-permute-start | bytes 442376 | tf_op jit(solution)/shard_map/ppermute | solution.py:22
  37.5 12.7 %collective-permute-start.9 = (bf16[768,384]{1,0:T(8,128)(2,1)S(1)}, bf16[768,384]{1,0:T(8,128)(2,1)S(1)}, u32[]{:S(2)}, u32[]{:S(2)}) collective-permute-start(bf16[768,384]{1,0:T(8,128)(2,1)S(1)} %copy-done.1), channel_id=1, source_target_pairs={{0,32},{32,64},{64,96},{96,128},{128,160},{160,192},{192,224},{224... | collective-permute-start | bytes 1769480 | tf_op jit(solution)/shard_map/ppermute | solution.py:22
  37.6 6.7 %collective-permute-start.8 = (bf16[2,96,384]{2,1,0:T(8,128)(2,1)S(1)}, bf16[2,96,384]{2,1,0:T(8,128)(2,1)S(1)}, u32[]{:S(2)}, u32[]{:S(2)}) collective-permute-start(bf16[2,96,384]{2,1,0:T(8,128)(2,1)S(1)} %bitcast_select_fusion.3), channel_id=1, source_target_pairs={{0,16},{16,0},{1,17},{17,1},{2,18},{18,2},{3,19},{19,3},{4,20},{20... | collective-permute-start | bytes 442376 | tf_op jit(solution)/shard_map/ppermute | solution.py:168
  52.4 31.4 %collective-permute-start.16 = (bf16[2,768,384]{2,1,0:T(8,128)(2,1)}, bf16[2,768,384]{2,1,0:T(8,128)(2,1)S(1)}, u32[]{:S(2)}, u32[]{:S(2)}) collective-permute-start(bf16[2,768,384]{2,1,0:T(8,128)(2,1)} %maximum_select_fusion), channel_id=1, source_target_pairs={{0,16},{16,0},{1,17},{17,1},{2,18},{18,2},{3,19},{19,3},{4,20},{20... | collective-permute-start | bytes 3538952 | tf_op jit(solution)/shard_map/ppermute | solution.py:171
  55.4 15.1 %collective-permute-start.10 = (bf16[2,96,384]{2,1,0:T(8,128)(2,1)S(1)}, bf16[2,96,384]{2,1,0:T(8,128)(2,1)S(1)}, u32[]{:S(2)}, u32[]{:S(2)}) collective-permute-start(bf16[2,96,384]{2,1,0:T(8,128)(2,1)S(1)} %broadcast_select_fusion.refs_2_), channel_id=1, source_target_pairs={{0,32},{32,64},{64,96},{96,128},{128,160},{160,192},{192,224},{224... | collective-permute-start | bytes 442376 | tf_op jit(solution)/shard_map/ppermute | solution.py:22
  55.4 15.8 %collective-permute-start.11 = (bf16[2,96,384]{2,1,0:T(8,128)(2,1)S(1)}, bf16[2,96,384]{2,1,0:T(8,128)(2,1)}, u32[]{:S(2)}, u32[]{:S(2)}) collective-permute-start(bf16[2,96,384]{2,1,0:T(8,128)(2,1)S(1)} %broadcast_select_fusion.refs_2_), channel_id=1, source_target_pairs={{0,224},{32,0},{64,32},{96,64},{128,96},{160,128},{192,160},{224,1... | collective-permute-start | bytes 442376 | tf_op jit(solution)/shard_map/ppermute | solution.py:22
  70.5 6.8 %collective-permute-start.12 = (bf16[2,96,384]{2,1,0:T(8,128)(2,1)S(1)}, bf16[2,96,384]{2,1,0:T(8,128)(2,1)S(1)}, u32[]{:S(2)}, u32[]{:S(2)}) collective-permute-start(bf16[2,96,384]{2,1,0:T(8,128)(2,1)S(1)} %collective-permute-done.10.refs_3_), channel_id=1, source_target_pairs={{0,32},{32,64},{64,96},{96,128},{128,160},{160,192},{192,224},{224... | collective-permute-start | bytes 442376 | tf_op jit(solution)/shard_map/ppermute | solution.py:22
  71.2 8.6 %collective-permute-start.13 = (bf16[2,96,384]{2,1,0:T(8,128)(2,1)}, bf16[2,96,384]{2,1,0:T(8,128)(2,1)}, u32[]{:S(2)}, u32[]{:S(2)}) collective-permute-start(bf16[2,96,384]{2,1,0:T(8,128)(2,1)} %collective-permute-done.11.refs_4_), channel_id=1, source_target_pairs={{0,224},{32,0},{64,32},{96,64},{128,96},{160,128},{192,160},{224,1... | collective-permute-start | bytes 442376 | tf_op jit(solution)/shard_map/ppermute | solution.py:22
  79.8 13.9 %collective-permute-start.15 = (bf16[2,96,384]{2,1,0:T(8,128)(2,1)}, bf16[2,96,384]{2,1,0:T(8,128)(2,1)S(1)}, u32[]{:S(2)}, u32[]{:S(2)}) collective-permute-start(bf16[2,96,384]{2,1,0:T(8,128)(2,1)} %collective-permute-done.13.refs_6_), channel_id=1, source_target_pairs={{0,224},{32,0},{64,32},{96,64},{128,96},{160,128},{192,160},{224,1... | collective-permute-start | bytes 442376 | tf_op jit(solution)/shard_map/ppermute | solution.py:22
  83.8 9.9 %collective-permute-start.17 = (bf16[2,96,384]{2,1,0:T(8,128)(2,1)}, bf16[2,96,384]{2,1,0:T(8,128)(2,1)S(1)}, u32[]{:S(2)}, u32[]{:S(2)}) collective-permute-start(bf16[2,96,384]{2,1,0:T(8,128)(2,1)} %collective-permute-done.14.refs_7_), channel_id=1, source_target_pairs={{0,32},{32,64},{64,96},{96,128},{128,160},{160,192},{192,224},{224... | collective-permute-start | bytes 442376 | tf_op jit(solution)/shard_map/ppermute | solution.py:22
  104.2 10.2 %collective-permute-start.24 = (bf16[2,48,1728]{2,1,0:T(8,128)(2,1)S(1)}, bf16[2,48,1728]{2,1,0:T(8,128)(2,1)S(1)}, u32[]{:S(2)}, u32[]{:S(2)}) collective-permute-start(bf16[2,48,1728]{2,1,0:T(8,128)(2,1)S(1)} %get-tuple-element.59), channel_id=1, source_target_pairs={{0,4},{4,8},{8,12},{12,0},{1,5},{5,9},{9,13},{13,1},{2,6},{6,10},{... | collective-permute-start | bytes 995336 | tf_op jit(solution)/shard_map/ppermute | solution.py:22
  106.6 24.7 %collective-permute-start.20 = (bf16[4,48,2688]{2,1,0:T(8,128)(2,1)S(1)}, bf16[4,48,2688]{2,1,0:T(8,128)(2,1)S(1)}, u32[]{:S(2)}, u32[]{:S(2)}) collective-permute-start(bf16[4,48,2688]{2,1,0:T(8,128)(2,1)S(1)} %bitcast.111), channel_id=1, source_target_pairs={{0,2},{2,0},{1,3},{3,1},{4,6},{6,4},{5,7},{7,5},{8,10},{10,8},{9,1... | collective-permute-start | bytes 3096584 | tf_op jit(solution)/shard_map/ppermute | solution.py:242
  107.3 10.9 %collective-permute-start.26 = (bf16[2,48,1728]{2,1,0:T(8,128)(2,1)S(1)}, bf16[2,48,1728]{2,1,0:T(8,128)(2,1)S(1)}, u32[]{:S(2)}, u32[]{:S(2)}) collective-permute-start(bf16[2,48,1728]{2,1,0:T(8,128)(2,1)S(1)} %get-tuple-element.60), channel_id=1, source_target_pairs={{0,12},{4,0},{8,4},{12,8},{1,13},{5,1},{9,5},{13,9},{2,14},{6,2},{... | collective-permute-start | bytes 995336 | tf_op jit(solution)/shard_map/ppermute | solution.py:22
  114.7 21.6 %collective-permute-start.25 = (bf16[2,48,3456]{2,1,0:T(8,128)(2,1)S(1)}, bf16[2,48,3456]{2,1,0:T(8,128)(2,1)S(1)}, u32[]{:S(2)}, u32[]{:S(2)}) collective-permute-start(bf16[2,48,3456]{2,1,0:T(8,128)(2,1)S(1)} %pad_maximum_fusion.1), channel_id=1, source_target_pairs={{0,4},{4,8},{8,12},{12,0},{1,5},{5,9},{9,13},{13,1},{2,6},{6,10},{... | collective-permute-start | bytes 1990664 | tf_op jit(solution)/shard_map/ppermute | solution.py:22
  118.5 17.7 %collective-permute-start.27 = (bf16[2,48,3456]{2,1,0:T(8,128)(2,1)S(1)}, bf16[2,48,3456]{2,1,0:T(8,128)(2,1)S(1)}, u32[]{:S(2)}, u32[]{:S(2)}) collective-permute-start(bf16[2,48,3456]{2,1,0:T(8,128)(2,1)S(1)} %pad_maximum_fusion.2), channel_id=1, source_target_pairs={{0,12},{4,0},{8,4},{12,8},{1,13},{5,1},{9,5},{13,9},{2,14},{6,2},{... | collective-permute-start | bytes 1990664 | tf_op jit(solution)/shard_map/ppermute | solution.py:22
  131.6 9.2 %collective-permute-start.21 = (bf16[48,2688]{1,0:T(8,128)(2,1)S(1)}, bf16[48,2688]{1,0:T(8,128)(2,1)S(1)}, u32[]{:S(2)}, u32[]{:S(2)}) collective-permute-start(bf16[48,2688]{1,0:T(8,128)(2,1)S(1)} %get-tuple-element.56), channel_id=1, source_target_pairs={{0,4},{4,8},{8,12},{12,0},{1,5},{5,9},{9,13},{13,1},{2,6},{6,10},{... | collective-permute-start | bytes 774152 | tf_op jit(solution)/shard_map/ppermute | solution.py:22
  133.2 13.6 %collective-permute-start.22 = (bf16[48,2688]{1,0:T(8,128)(2,1)S(1)}, bf16[48,2688]{1,0:T(8,128)(2,1)S(1)}, u32[]{:S(2)}, u32[]{:S(2)}) collective-permute-start(bf16[48,2688]{1,0:T(8,128)(2,1)S(1)} %get-tuple-element.58), channel_id=1, source_target_pairs={{0,12},{4,0},{8,4},{12,8},{1,13},{5,1},{9,5},{13,9},{2,14},{6,2},{... | collective-permute-start | bytes 774152 | tf_op jit(solution)/shard_map/ppermute | solution.py:22
  133.7 13.0 %collective-permute-start.23 = (bf16[48,2688]{1,0:T(8,128)(2,1)S(1)}, bf16[48,2688]{1,0:T(8,128)(2,1)S(1)}, u32[]{:S(2)}, u32[]{:S(2)}) collective-permute-start(bf16[48,2688]{1,0:T(8,128)(2,1)S(1)} %get-tuple-element.57), channel_id=1, source_target_pairs={{0,8},{4,12},{8,0},{12,4},{1,9},{5,13},{9,1},{13,5},{2,10},{6,14},... | collective-permute-start | bytes 774152 | tf_op jit(solution)/shard_map/ppermute | solution.py:22
  136.4 10.5 %collective-permute-start.28 = (bf16[48,3456]{1,0:T(8,128)(2,1)S(1)}, bf16[48,3456]{1,0:T(8,128)(2,1)S(1)}, u32[]{:S(2)}, u32[]{:S(2)}) collective-permute-start(bf16[48,3456]{1,0:T(8,128)(2,1)S(1)} %fusion.5), channel_id=1, source_target_pairs={{0,2},{2,0},{1,3},{3,1},{4,6},{6,4},{5,7},{7,5},{8,10},{10,8},{9,1... | collective-permute-start | bytes 995336 | tf_op jit(solution)/shard_map/ppermute | solution.py:246
  (24 other events, 244.9 us)
